TPU v7x, 512 devices: a whole 4x4x16 slice. The times are simulated.
512 devices in a mesh: sec: 16 (over y_lo, x, core), sp: 16 (over z), tp: 2 (over y_hi).
Axes of the slice: x: 4, y: 4 (y_hi: 2, y_lo: 2; y = y_hi * 2 + y_lo), z: 16, core: 2. Of those that a mesh axis runs over, the one named last changes fastest.
Arguments:
- text_hidden: bfloat16 [32, 256, 3072], P('sec', 'sp', 'tp'), may hold values from -6 to 6
- text_qkv_weight: bfloat16 [3072, 16, 384], P('tp', 'sp'), may hold values from -0.109375 to 0.109375
- image_qkv: bfloat16 [32, 2048, 16, 384], P(('sec', 'tp'), 'sp'), may hold values from -8 to 8
- mod_weight: float32 [256, 16, 128], P(None, 'sp'), may hold values from -0.375 to 0.375
- lengths: int32 [32], P(('sec', 'tp')), may hold values from 32 to 256
- timesteps: int32 [32], P(('sec', 'tp')), may hold values from 0 to 999
Outputs:
- image_out: bfloat16 [32, 2048, 16, 128], P(('sec', 'tp'), 'sp')
- text_out: bfloat16 [32, 256, 16, 128], P(('sec', 'tp'), None, 'sp')
All inputs are finite; a program needn't handle non-finite values.
Results may differ from a plain program's by a relative error of at most 0.0077.
Values may be sent and summed in bfloat16 or wider, within the bound.
No kernel may reach another device: no remote copies, remote signals or barrier semaphores. Data moves between devices by JAX's collectives and lax.ppermute only.
A program may use at most 64 MiB of HBM per device.

v0:
```python
import math

import jax
import jax.numpy as jnp
from jax import lax
from jax.sharding import PartitionSpec as P


def from_behind(x, axis, by):
    count = lax.axis_size(axis)
    return lax.ppermute(x, axis, [(i, (i + by) % count) for i in range(count)])


def pick_block(row_count):
    options = [size for size in range(512, row_count + 1) if row_count % size == 0]
    return options[0]


def gate_of(timestep, mod_weight):
    width = mod_weight.shape[0]
    half_width = width // 2
    frequency = jnp.exp(-math.log(10000.0) * jnp.arange(half_width, dtype=jnp.float32) / half_width)
    angles = timestep.astype(jnp.float32) * frequency
    embedding = jnp.concatenate([jnp.cos(angles), jnp.sin(angles)])
    flat = mod_weight.reshape(width, -1)
    gate_scale = jnp.dot(embedding[None, :], flat, precision=lax.Precision.HIGHEST)
    return gate_scale


def attend(joint, length, text_rows, gate_scale):
    row_count = joint.shape[0]
    head_count = joint.shape[1]
    head_size = gate_scale.shape[1]
    queries = joint[:, :, :head_size]
    key_rows = joint[:, :, head_size : 2 * head_size]
    value_rows = joint[:, :, 2 * head_size :]
    block_rows = pick_block(row_count)
    position = jnp.arange(row_count)
    key_valid = (position >= text_rows) | (position < length)
    score_scale = 1.0 / math.sqrt(head_size)
    query_blocks = queries.reshape(row_count // block_rows, block_rows, head_count, head_size)

    def one_block(query_block):
        scores = (
            jnp.einsum("qhc,khc->hqk", query_block, key_rows, preferred_element_type=jnp.float32)
            * score_scale
        )
        scores = jnp.where(key_valid[None, None, :], scores, -jnp.inf)
        largest = jnp.max(scores, axis=-1, keepdims=True)
        expo = jnp.exp(scores - largest)
        weights = (expo / jnp.sum(expo, axis=-1, keepdims=True)).astype(jnp.bfloat16)
        output = jnp.einsum("hqk,khc->qhc", weights, value_rows, preferred_element_type=jnp.float32)
        return (output * gate_scale[None, :, :]).astype(jnp.bfloat16)

    return lax.map(one_block, query_blocks).reshape(row_count, head_count, head_size)


def shards(text_hidden, text_qkv_weight, image_qkv, mod_weight, lengths, timesteps):
    relayed = from_behind(text_hidden, "sec", lax.axis_size("sec") // 2)
    partial_terms = jnp.einsum(
        "srd,dhc->srhc",
        lax.all_gather(relayed, "sp", axis=1, tiled=True),
        text_qkv_weight,
        preferred_element_type=jnp.float32,
    )
    text_qkv = lax.psum_scatter(partial_terms, "tp", scatter_dimension=0, tiled=True).astype(
        jnp.bfloat16
    )
    head_image = lax.all_to_all(image_qkv, "sp", split_axis=2, concat_axis=1, tiled=True)
    text_count = text_qkv.shape[1]
    joint = jnp.concatenate([text_qkv, head_image], axis=1)[0]
    gate_scale = gate_of(timesteps[0], mod_weight)
    attended = attend(joint, lengths[0], text_count, gate_scale)
    text_out = attended[:text_count][None]
    image_heads = attended[text_count:][None]
    image_out = lax.all_to_all(image_heads, "sp", split_axis=1, concat_axis=2, tiled=True)
    return (image_out, text_out)


def solution(mesh):
    in_specs = (
        P("sec", "sp", "tp"),
        P("tp", "sp", None),
        P(("sec", "tp"), "sp", None, None),
        P(None, "sp", None),
        P(("sec", "tp")),
        P(("sec", "tp")),
    )
    out_specs = (P(("sec", "tp"), "sp", None, None), P(("sec", "tp"), None, "sp", None))
    return jax.shard_map(shards, mesh=mesh, in_specs=in_specs, out_specs=out_specs, check_vma=False)
```

profile of v0, /device:TPU:2, one launch (start us, length us, event | category | flops | bytes accessed | tf_op | source)
XLA Modules:
  0.0 248.2 jit_solution(15650738528937105945)
XLA Ops:
  7.2 0.0 copy-start
  7.2 0.0 copy-start.3
  7.2 3.0 %copy.19 = bf16[1,128,16,384]{3,1,0,2:T(8,128)(2,1)} copy(bf16[1,128,16,384]{3,2,1,0:T(8,128)(2,1)} %param.10) | data formatting | bytes 3145728 | tf_op args[2]
  10.2 0.0 copy-start.1
  10.2 15.3 %all-to-all-start = ((bf16[1,128,16,384]{3,1,0,2:T(8,128)(2,1)}), bf16[1,128,16,384]{3,1,0,2:T(8,128)(2,1)S(1)}, u32[]{:S(2)}, u32[]{:S(2)}) async-start(bf16[1,128,16,384]{3,1,0,2:T(8,128)(2,1)} %copy.19), calls=%async_computation.1 | async-start | bytes 3145728 | tf_op jit(solution)/shard_map/all_to_all | solution.py:69
  25.6 0.0 all-gather.2.cloned.1.call-start
  25.6 0.0 copy-done.3
  25.6 3.5 %collective-permute-start = (bf16[2,16,1536]{2,1,0:T(8,128)(2,1)S(1)}, bf16[2,16,1536]{2,1,0:T(8,128)(2,1)S(1)}, u32[]{:S(2)}, u32[]{:S(2)}) collective-permute-start(bf16[2,16,1536]{2,1,0:T(8,128)(2,1)S(1)} %copy-done.3), channel_id=1, source_target_pairs={{0,256},{32,288},{64,320},{96,352},{128,384},{160,416},{192,448},{... | collective-permute-start | bytes 294920 | tf_op jit(solution)/shard_map/ppermute | solution.py:11
  29.1 3.0 %collective-permute-done = bf16[2,16,1536]{2,1,0:T(8,128)(2,1)S(1)} collective-permute-done((bf16[2,16,1536]{2,1,0:T(8,128)(2,1)S(1)}, bf16[2,16,1536]{2,1,0:T(8,128)(2,1)S(1)}, u32[]{:S(2)}, u32[]{:S(2)}) %collective-permute-start) | collective-permute-done | bytes 98336 | tf_op jit(solution)/shard_map/ppermute | solution.py:11
  32.1 0.0 copy-start.2
  32.1 0.6 copy-done.2
  32.8 0.0 all-gather.2.cloned.1.call-update
  32.8 0.0 reduce-scatter.2.cloned.1.call-start
  32.9 99.4 %all-gather.2.cloned.1.call-done = bf16[2,256,1536]{2,1,0:T(8,128)(2,1)} async-done(((bf16[2,16,1536]{2,1,0:T(8,128)(2,1)}), bf16[2,256,1536]{2,1,0:T(8,128)(2,1)}) %all-gather.2.cloned.1.call-update) | async-done | bytes 1572880 | tf_op jit(solution)/shard_map/all_gather | solution.py:62
  132.2 0.0 copy-done
  132.2 3.3 %convolution_bitcast_fusion = f32[2,256,1,384]{3,1,0,2:T(8,128)} fusion(bf16[2,256,1536]{2,1,0:T(8,128)(2,1)} %all-gather.2.cloned.1.call-done, bf16[1536,1,384]{2,0,1:T(8,128)(2,1)S(1)} %copy-done), kind=kOutput, calls=%fused_computation.20 | convolution fusion | flops 603979776 | bytes 3538944 | tf_op jit(solution)/shard_map/srd,dhc->srhc/dot_general | solution.py:60
  135.5 0.0 reduce-scatter.2.cloned.1.call-update
  136.3 0.0 copy-done.1
  136.3 0.2 fusion.20
  136.4 24.6 %reduce-scatter.2.cloned.1.call-done = f32[1,256,1,384]{3,1,0,2:T(8,128)} async-done(((f32[2,256,1,384]{3,1,0,2:T(8,128)}), f32[1,256,1,384]{3,1,0,2:T(8,128)}) %reduce-scatter.2.cloned.1.call-update) | async-done | bytes 393232 | tf_op jit(solution)/shard_map/reduce_scatter | solution.py:66
  161.1 1.0 convert_bitcast_fusion
  162.1 0.0 all-to-all-done
  162.1 0.2 maximum_bitcast_fusion
  162.3 0.3 fusion.19
  162.6 14.5 %while.11 = (s32[]{:T(128)}, bf16[4,576,1,128]{3,1,2,0:T(8,128)(2,1)S(1)}, bf16[4,576,1,128]{3,1,2,0:T(8,128)(2,1)S(1)}, bf16[2304,1,128]{2,0,1:T(8,128)(2,1)S(1...) while((s32[]{:T(128)}, ...), condition=%wide.region_4.5_spmd.clone, body=%wide.region_1.4_spmd.clone.sunk | while | flops 690247296 | bytes 17420896 | solution.py:55
  162.6 0.7 fusion.30
  163.3 1.0 fusion.31
  164.3 0.9 fusion.32
  165.2 1.1 fusion.33
  166.2 0.7 fusion.30
  166.9 1.0 fusion.31
  167.9 0.9 fusion.32
  168.8 1.1 fusion.33
  169.9 0.7 fusion.30
  170.5 1.0 fusion.31
  171.5 0.9 fusion.32
  172.4 1.1 fusion.33
  173.5 0.7 fusion.30
  174.2 1.0 fusion.31
  175.2 0.9 fusion.32
  176.0 1.1 fusion.33
  177.2 8.1 %copy.26 = bf16[1,2048,1,128]{3,2,0,1:T(2,128)(2,1)S(1)} copy(bf16[1,2048,1,128]{3,1,2,0:T(8,128)(2,1)S(1)} %slice_bitcast_fusion) | data formatting | bytes 1048576 | tf_op jit(solution)/shard_map/broadcast_in_dim | solution.py:75
  185.3 0.5 broadcast.20
  185.8 11.5 %reduce.4 = bf16[2048,128]{1,0:T(8,128)(2,1)S(1)} reduce(bf16[2048,1,1,128]{3,2,1,0:T(2,128)(2,1)S(1)} %bitcast.86, bf16[]{:T(256)} %broadcast.20), dimensions={1,2}, to_apply=%bitcast.71.reduce_sub_computation | reduce | bytes 1048578
  197.4 0.9 reshape.67
  198.3 12.3 %all-to-all-start.1 = ((bf16[16,2,8192]{2,1,0:T(2,128)(2,1)}), bf16[16,2,8192]{2,1,0:T(2,128)(2,1)S(1)}, u32[]{:S(2)}, u32[]{:S(2)}) async-start(bf16[16,2,8192]{2,1,0:T(2,128)(2,1)} %reshape.67), calls=%async_computation.2 | async-start | bytes 1048576 | tf_op jit(solution)/shard_map/all_to_all | solution.py:76
  210.5 0.6 slice_bitcast_fusion.1
  211.2 28.5 %all-to-all-done.1 = bf16[16,2,8192]{2,1,0:T(2,128)(2,1)S(1)} async-done(((bf16[16,2,8192]{2,1,0:T(2,128)(2,1)}), bf16[16,2,8192]{2,1,0:T(2,128)(2,1)S(1)}, u32[]{:S(2)}, u32[]{:S(2)}) %all-to-all-start.1) | async-done | bytes 524320 | tf_op jit(solution)/shard_map/all_to_all | solution.py:76
  239.6 0.5 reshape.68
  240.2 0.1 copy.24
  240.2 1.1 copy.23
  (4 shorter events, 0.1 us)
Async XLA Ops:
  7.2 125.1 %copy-start = (bf16[1536,1,384]{2,0,1:T(8,128)(2,1)S(1)}, bf16[1536,1,384]{2,0,1:T(8,128)(2,1)}, u32[]{:S(2)}) copy-start(bf16[1536,1,384]{2,0,1:T(8,128)(2,1)} %param.9) | copy-start | bytes 3538948
  7.2 18.4 %copy-start.3 = (bf16[2,16,1536]{2,1,0:T(8,128)(2,1)S(1)}, bf16[2,16,1536]{2,1,0:T(8,128)(2,1)}, u32[]{:S(2)}) copy-start(bf16[2,16,1536]{2,1,0:T(8,128)(2,1)} %param.8) | copy-start | bytes 294916
  10.2 126.0 %copy-start.1 = (f32[256,1,128]{2,1,0:T(1,128)S(1)}, f32[256,1,128]{2,1,0:T(1,128)}, u32[]{:S(2)}) copy-start(f32[256,1,128]{2,1,0:T(1,128)} %param.11) | copy-start | bytes 393220
  10.2 151.9 %all-to-all-start = ((bf16[1,128,16,384]{3,1,0,2:T(8,128)(2,1)}), bf16[1,128,16,384]{3,1,0,2:T(8,128)(2,1)S(1)}, u32[]{:S(2)}, u32[]{:S(2)}) async-start(bf16[1,128,16,384]{3,1,0,2:T(8,128)(2,1)} %copy.19), calls=%async_computation.1 | async-start | bytes 3145728 | tf_op jit(solution)/shard_map/all_to_all | solution.py:69
  25.6 106.7 %all-gather.2.cloned.1.call-start = ((), (), s32[]{:S(2)}) async-start(), calls=%async_computation.3 | async-start | bytes 1671168 | tf_op jit(solution)/shard_map/all_gather | solution.py:62
  25.6 6.5 %collective-permute-start = (bf16[2,16,1536]{2,1,0:T(8,128)(2,1)S(1)}, bf16[2,16,1536]{2,1,0:T(8,128)(2,1)S(1)}, u32[]{:S(2)}, u32[]{:S(2)}) collective-permute-start(bf16[2,16,1536]{2,1,0:T(8,128)(2,1)S(1)} %copy-done.3), channel_id=1, source_target_pairs={{0,256},{32,288},{64,320},{96,352},{128,384},{160,416},{192,448},{... | collective-permute-start | bytes 294920 | tf_op jit(solution)/shard_map/ppermute | solution.py:11
  32.1 0.6 copy-start.2
  32.8 128.3 %reduce-scatter.2.cloned.1.call-start = ((), (), s32[]{:S(2)}) async-start(), calls=%async_computation.4 | async-start | bytes 1179648 | tf_op jit(solution)/shard_map/reduce_scatter | solution.py:66
  198.3 41.4 %all-to-all-start.1 = ((bf16[16,2,8192]{2,1,0:T(2,128)(2,1)}), bf16[16,2,8192]{2,1,0:T(2,128)(2,1)S(1)}, u32[]{:S(2)}, u32[]{:S(2)}) async-start(bf16[16,2,8192]{2,1,0:T(2,128)(2,1)} %reshape.67), calls=%async_computation.2 | async-start | bytes 1048576 | tf_op jit(solution)/shard_map/all_to_all | solution.py:76
Sparse Core Ops, SparseCore 0:
  32.9 99.2 all-gather.1
  135.7 25.3 reduce-scatter.1
where the time goes:
time: 249 us; the launch traced here: 248 us
  waiting for transfers between devices  156 us (63%)
  starting transfers between devices  31.2 us (13%)
  other arithmetic  18.9 us (8%)
  local copies, waits for them, and re-layouts  16 us (6%)
  between operations  14.8 us (6%)
  matrix products  11.8 us (5%)
    all_gather x1, waiting for transfers between devices, shards(): lax.all_gather(relayed, 'sp', axis=1, tiled=True)  99.4 us
    all_to_all x1, waiting for transfers between devices, shards(): lax.all_to_all(image_heads, 'sp', split_axis=1, concat_axis=2, tiled=True)  28.5 us
    reduce_scatter x1, waiting for transfers between devices, shards(): lax.psum_scatter(partial_terms, 'tp', scatter_dimension=0, tiled=True)  24.6 us
    all_to_all x1, starting transfers between devices, shards(): lax.all_to_all(image_qkv, 'sp', split_axis=2, concat_axis=1, tiled=True)  15.3 us
    all_to_all x1, starting transfers between devices, shards(): lax.all_to_all(image_heads, 'sp', split_axis=1, concat_axis=2, tiled=True)  12.3 us
    unnamed x1, other arithmetic  11.5 us
    broadcast_in_dim x2, local copies, waits for them, and re-layouts, shards(): image_heads = attended[text_count:][None]  8.17 us
    unnamed x14, local copies, waits for them, and re-layouts  6.85 us
  transfers between devices with their start and end apart: 5, of which 4 were waited for; matrix products, arithmetic and copies ran while one was open for 2% of the time, Pallas kernels for 0%

commit v1 on v0

v1 whole, which is shorter than its diff:
```python
import functools
import math

import jax
import jax.numpy as jnp
from jax import lax
from jax.experimental import pallas as pl
from jax.experimental.pallas import tpu as pltpu
from jax.sharding import PartitionSpec as P

TRANSPOSED = (((1,), (1,)), ((), ()))


def gate_of(timestep, mod_weight):
    width = mod_weight.shape[0]
    half_width = width // 2
    frequency = jnp.exp(-math.log(10000.0) * jnp.arange(half_width, dtype=jnp.float32) / half_width)
    angles = timestep.astype(jnp.float32) * frequency
    embedding = jnp.concatenate([jnp.cos(angles), jnp.sin(angles)])
    flat = mod_weight.reshape(width, -1)
    return jnp.dot(embedding[None, :], flat, precision=lax.Precision.HIGHEST)


def attend_kernel(length_ref, image_ref, text_ref, gate_ref, image_out, text_out, *, rows, unroll):
    head = gate_ref.shape[1]
    text_count = text_ref.shape[0]
    block_count = image_ref.shape[0] // (rows * unroll)
    scale = math.log2(math.e) / math.sqrt(head)
    text_keys = text_ref[:, head : 2 * head]
    image_keys = image_ref[:, head : 2 * head]
    text_values = text_ref[:, 2 * head :]
    text_values = jnp.concatenate([text_values, jnp.ones_like(text_values)], axis=1)
    image_values = image_ref[:, 2 * head :]
    image_values = jnp.concatenate([image_values, jnp.ones_like(image_values)], axis=1)
    gate = gate_ref[...]
    position = lax.broadcasted_iota(jnp.int32, (1, text_count), 1)
    excluded = jnp.where(position < length_ref[0], 0.0, -jnp.inf)

    def one_block(queries):
        text_scores = lax.dot_general(
            queries, text_keys, TRANSPOSED, preferred_element_type=jnp.float32
        )
        text_scores = text_scores + excluded
        image_scores = lax.dot_general(
            queries, image_keys, TRANSPOSED, preferred_element_type=jnp.float32
        )
        largest = jnp.maximum(
            jnp.max(text_scores, axis=-1, keepdims=True),
            jnp.max(image_scores, axis=-1, keepdims=True),
        )
        text_weights = jnp.exp2((text_scores - largest) * scale).astype(jnp.bfloat16)
        image_weights = jnp.exp2((image_scores - largest) * scale).astype(jnp.bfloat16)
        total = jnp.dot(text_weights, text_values, preferred_element_type=jnp.float32)
        total = total + jnp.dot(image_weights, image_values, preferred_element_type=jnp.float32)
        return (total[:, :head] * (gate / total[:, head:])).astype(jnp.bfloat16)

    step = pl.program_id(0)

    @pl.when(step < block_count)
    def _():
        for part in range(unroll):
            at = pl.ds(pl.multiple_of((step * unroll + part) * rows, rows), rows)
            image_out[at, :] = one_block(image_ref[at, :head])

    @pl.when(step == block_count)
    def _():
        text_out[...] = one_block(text_ref[:, :head])


def attend(image, text, length, gate_scale):
    image_count, width = image.shape
    text_count = text.shape[0]
    head = width // 3
    rows, unroll = 512, 2
    whole = lambda shape: pl.BlockSpec(shape, lambda i: (0, 0))
    return pl.pallas_call(
        functools.partial(attend_kernel, rows=rows, unroll=unroll),
        grid=(image_count // (rows * unroll) + 1,),
        in_specs=[
            pl.BlockSpec(memory_space=pltpu.SMEM),
            whole((image_count, width)),
            whole((text_count, width)),
            whole((1, head)),
        ],
        out_specs=[whole((image_count, head)), whole((text_count, head))],
        out_shape=[
            jax.ShapeDtypeStruct((image_count, head), jnp.bfloat16),
            jax.ShapeDtypeStruct((text_count, head), jnp.bfloat16),
        ],
        compiler_params=pltpu.CompilerParams(vmem_limit_bytes=48 * 2**20),
    )(length, image, text, gate_scale)


def shards(text_hidden, text_qkv_weight, image_qkv, mod_weight, lengths, timesteps):
    sec, sp, tp = (lax.axis_size(axis) for axis in ("sec", "sp", "tp"))
    mine = lax.axis_index("tp")
    other = 1 - mine

    def to_group(x, flip):
        moves = [
            (s * tp + t, ((s + sec // 2) % sec) * tp + (t + flip) % tp)
            for s in range(sec)
            for t in range(tp)
        ]
        return lax.ppermute(x, ("sec", "tp"), moves)

    near = to_group(lax.dynamic_index_in_dim(text_hidden, mine, 0, keepdims=False), 0)
    far = to_group(lax.dynamic_index_in_dim(text_hidden, other, 0, keepdims=False), 1)
    halves = lax.all_gather(jnp.stack([near, far]), "sp", axis=1, tiled=True)
    own_weight = text_qkv_weight[:, 0]
    other_weight = lax.ppermute(own_weight, "tp", [(0, 1), (1, 0)])

    by_head = image_qkv[0].transpose(1, 0, 2)
    image = lax.all_to_all(by_head, "sp", split_axis=0, concat_axis=0)
    heads, rows, width = image.shape
    gate_scale = gate_of(timesteps[0], mod_weight)

    text = jnp.dot(halves[0], own_weight, preferred_element_type=jnp.float32)
    text = text + jnp.dot(halves[1], other_weight, preferred_element_type=jnp.float32)
    image_heads, text_out = attend(
        image.reshape(heads * rows, width), text.astype(jnp.bfloat16), lengths, gate_scale
    )
    image_out = lax.all_to_all(
        image_heads.reshape(sp, rows, width // 3), "sp", split_axis=0, concat_axis=0
    )
    return (image_out.transpose(1, 0, 2)[None], text_out[None, :, None, :])


def solution(mesh):
    in_specs = (
        P("sec", "sp", "tp"),
        P("tp", "sp", None),
        P(("sec", "tp"), "sp", None, None),
        P(None, "sp", None),
        P(("sec", "tp")),
        P(("sec", "tp")),
    )
    out_specs = (P(("sec", "tp"), "sp", None, None), P(("sec", "tp"), None, "sp", None))
    return jax.shard_map(shards, mesh=mesh, in_specs=in_specs, out_specs=out_specs, check_vma=False)
```

time: 249 us -> 187 us (0.75)
  the two profiles are of different devices: /device:TPU:2 before, /device:TPU:12 now
where the time goes in v1:
time: 187 us
  waiting for transfers between devices  93.2 us (50%)
  blocking collectives  31.9 us (17%)
  starting transfers between devices  27.4 us (15%)
  between operations  15.5 us (8%)
  Pallas kernels  10.5 us (6%)
  local copies, waits for them, and re-layouts  4.16 us (2%)
  matrix products  3.83 us (2%)
    all_gather x1, waiting for transfers between devices, shards(): halves = lax.all_gather(jnp.stack([near, far]), 'sp', axis=1, tiled=True)  91.1 us
    all_to_all x1, blocking collectives, shards(): lax.all_to_all(image_heads.reshape(sp, rows, width // 3), 'sp', split_axi...  31.9 us
    all_to_all x1, starting transfers between devices, shards(): image = lax.all_to_all(by_head, 'sp', split_axis=0, concat_axis=0)  15.3 us
    pallas_call x1, Pallas kernels, attend(): pl.pallas_call(functools.partial(attend_kernel, rows=rows, unroll=unroll)...  10.5 us
    ppermute x2, starting transfers between devices, to_group(): return lax.ppermute(x, ('sec', 'tp'), moves)  6.68 us
    ppermute x1, starting transfers between devices, shards(): other_weight = lax.ppermute(own_weight, 'tp', [(0, 1), (1, 0)])  5.31 us
    unnamed x10, local copies, waits for them, and re-layouts  4.14 us
  transfers between devices with their start and end apart: 5, of which 2 were waited for; matrix products, arithmetic and copies ran while one was open for 2% of the time, Pallas kernels for 0%

profile of v1, /device:TPU:12, one launch (start us, length us, event | category | flops | bytes accessed | tf_op | source)
XLA Modules:
  0.0 187.0 jit_solution(8011043086120024222)
XLA Ops:
  7.2 0.0 copy-start
  7.2 3.0 %copy.13 = bf16[1,128,16,384]{3,1,2,0:T(8,128)(2,1)} copy(bf16[1,128,16,384]{3,2,1,0:T(8,128)(2,1)} %param.8) | data formatting | bytes 3145728 | tf_op args[2]
  10.2 0.0 copy-start.1
  10.2 0.0 copy-start.3
  10.2 15.3 %all-to-all-start = ((bf16[16,128,384]{2,1,0:T(8,128)(2,1)}), bf16[16,128,384]{2,1,0:T(8,128)(2,1)S(1)}, u32[]{:S(2)}, u32[]{:S(2)}) async-start(bf16[16,128,384]{2,1,0:T(8,128)(2,1)} %bitcast.32), calls=%async_computation | async-start | bytes 3145728 | tf_op jit(solution)/shard_map/all_to_all | solution.py:114
  25.5 0.0 all-gather.2.cloned.1.call-start
  25.6 0.0 copy-done.1
  25.6 2.4 %collective-permute-start = (bf16[16,1536]{1,0:T(8,128)(2,1)S(1)}, bf16[16,1536]{1,0:T(8,128)(2,1)S(1)}, u32[]{:S(2)}, u32[]{:S(2)}) collective-permute-start(bf16[16,1536]{1,0:T(8,128)(2,1)S(1)} %get-tuple-element.8), channel_id=1, source_target_pairs={{0,256},{1,257},{32,288},{33,289},{64,320},{65,321},{96,352},{97,3... | collective-permute-start | bytes 147464 | tf_op jit(solution)/shard_map/ppermute | solution.py:105
  28.0 4.3 %collective-permute-start.1 = (bf16[16,1536]{1,0:T(8,128)(2,1)S(1)}, bf16[16,1536]{1,0:T(8,128)(2,1)S(1)}, u32[]{:S(2)}, u32[]{:S(2)}) collective-permute-start(bf16[16,1536]{1,0:T(8,128)(2,1)S(1)} %get-tuple-element.9), channel_id=1, source_target_pairs={{0,257},{1,256},{32,289},{33,288},{64,321},{65,320},{96,353},{97,3... | collective-permute-start | bytes 147464 | tf_op jit(solution)/shard_map/ppermute | solution.py:105
  32.3 0.0 collective-permute-done
  32.3 2.0 %collective-permute-done.1 = bf16[16,1536]{1,0:T(8,128)(2,1)S(1)} collective-permute-done((bf16[16,1536]{1,0:T(8,128)(2,1)S(1)}, bf16[16,1536]{1,0:T(8,128)(2,1)S(1)}, u32[]{:S(2)}, u32[]{:S(2)}) %collective-permute-start.1) | collective-permute-done | bytes 49184 | tf_op jit(solution)/shard_map/ppermute | solution.py:105
  34.3 0.7 pad_maximum_fusion
  35.0 0.0 all-gather.2.cloned.1.call-update
  35.0 0.0 copy-done.3
  35.0 5.3 %collective-permute-start.2 = (bf16[1536,384]{1,0:T(8,128)(2,1)S(1)}, bf16[1536,384]{1,0:T(8,128)(2,1)}, u32[]{:S(2)}, u32[]{:S(2)}) collective-permute-start(bf16[1536,384]{1,0:T(8,128)(2,1)S(1)} %bitcast.40), channel_id=1, source_target_pairs={{0,1},{1,0},{2,3},{3,2},{4,5},{5,4},{6,7},{7,6},{8,9},{9,8},{10,11... | collective-permute-start | bytes 3538952 | tf_op jit(solution)/shard_map/ppermute | solution.py:111
  41.7 0.0 copy-done
  41.7 0.2 fusion.5.gate_ref
  41.9 91.1 %all-gather.2.cloned.1.call-done = bf16[2,256,1536]{2,1,0:T(8,128)(2,1)} async-done(((bf16[2,16,1536]{2,1,0:T(8,128)(2,1)}), bf16[2,256,1536]{2,1,0:T(8,128)(2,1)}) %all-gather.2.cloned.1.call-update) | async-done | bytes 1572880 | tf_op jit(solution)/shard_map/all_gather | solution.py:109
  133.0 0.0 copy-start.2
  133.0 1.8 fusion.1
  134.8 0.0 collective-permute-done.2
  134.8 0.0 copy-done.2
  134.8 1.8 fusion.text_ref
  136.7 0.0 all-to-all-done
  136.7 10.5 %shard_map.77 = (bf16[2048,128]{1,0:T(8,128)(2,1)S(1)}, bf16[256,128]{1,0:T(8,128)(2,1)}) custom-call(s32[1]{0:T(128)S(6)} %copy.14.length_ref, bf16[2048,384]{1,0:T(8,128)(2,1)S(1)} %bitcast.34, bf16[256,384]{1,0:T(8,128)(2,1)S(1)} %fusion.text_ref, f32[1,128]{1,0:T(1,128)S(1)} %fusion.5.gate_ref), custom_call_target="tpu_custom_call" | custom-call | tf_op jit(solution)/shard_map/pallas_call | solution.py:76
  147.2 31.9 %all_to_all.10 = bf16[16,128,128]{2,1,0:T(8,128)(2,1)S(1)} all-to-all(bf16[16,128,128]{2,1,0:T(8,128)(2,1)S(1)} %bitcast.35), channel_id=1, replica_groups=mesh['sec'=16,'sp'=16,'tp'=2] {'sp'}, dimensions={0} | all-to-all | bytes 1048576 | tf_op jit(solution)/shard_map/all_to_all | solution.py:123
  179.1 1.1 copy.11
  (3 shorter events, 0.1 us)
Async XLA Ops:
  7.2 34.5 %copy-start = (f32[256,1,128]{2,1,0:T(1,128)S(1)}, f32[256,1,128]{2,1,0:T(1,128)}, u32[]{:S(2)}) copy-start(f32[256,1,128]{2,1,0:T(1,128)} %param.9) | copy-start | bytes 393220
  10.2 15.4 %copy-start.1 = (bf16[2,16,1536]{2,1,0:T(8,128)(2,1)S(1)}, bf16[2,16,1536]{2,1,0:T(8,128)(2,1)}, u32[]{:S(2)}) copy-start(bf16[2,16,1536]{2,1,0:T(8,128)(2,1)} %param.6) | copy-start | bytes 294916
  10.2 24.8 %copy-start.3 = (bf16[1536,1,384]{2,0,1:T(8,128)(2,1)S(1)}, bf16[1536,1,384]{2,0,1:T(8,128)(2,1)}, u32[]{:S(2)}) copy-start(bf16[1536,1,384]{2,0,1:T(8,128)(2,1)} %param.7) | copy-start | bytes 3538948
  10.2 126.5 %all-to-all-start = ((bf16[16,128,384]{2,1,0:T(8,128)(2,1)}), bf16[16,128,384]{2,1,0:T(8,128)(2,1)S(1)}, u32[]{:S(2)}, u32[]{:S(2)}) async-start(bf16[16,128,384]{2,1,0:T(8,128)(2,1)} %bitcast.32), calls=%async_computation | async-start | bytes 3145728 | tf_op jit(solution)/shard_map/all_to_all | solution.py:114
  25.5 107.5 %all-gather.2.cloned.1.call-start = ((), (), s32[]{:S(2)}) async-start(), calls=%async_computation.2 | async-start | bytes 1671168 | tf_op jit(solution)/shard_map/all_gather | solution.py:109
  25.6 6.7 %collective-permute-start = (bf16[16,1536]{1,0:T(8,128)(2,1)S(1)}, bf16[16,1536]{1,0:T(8,128)(2,1)S(1)}, u32[]{:S(2)}, u32[]{:S(2)}) collective-permute-start(bf16[16,1536]{1,0:T(8,128)(2,1)S(1)} %get-tuple-element.8), channel_id=1, source_target_pairs={{0,256},{1,257},{32,288},{33,289},{64,320},{65,321},{96,352},{97,3... | collective-permute-start | bytes 147464 | tf_op jit(solution)/shard_map/ppermute | solution.py:105
  28.0 6.4 %collective-permute-start.1 = (bf16[16,1536]{1,0:T(8,128)(2,1)S(1)}, bf16[16,1536]{1,0:T(8,128)(2,1)S(1)}, u32[]{:S(2)}, u32[]{:S(2)}) collective-permute-start(bf16[16,1536]{1,0:T(8,128)(2,1)S(1)} %get-tuple-element.9), channel_id=1, source_target_pairs={{0,257},{1,256},{32,289},{33,288},{64,321},{65,320},{96,353},{97,3... | collective-permute-start | bytes 147464 | tf_op jit(solution)/shard_map/ppermute | solution.py:105
  35.0 99.8 %collective-permute-start.2 = (bf16[1536,384]{1,0:T(8,128)(2,1)S(1)}, bf16[1536,384]{1,0:T(8,128)(2,1)}, u32[]{:S(2)}, u32[]{:S(2)}) collective-permute-start(bf16[1536,384]{1,0:T(8,128)(2,1)S(1)} %bitcast.40), channel_id=1, source_target_pairs={{0,1},{1,0},{2,3},{3,2},{4,5},{5,4},{6,7},{7,6},{8,9},{9,8},{10,11... | collective-permute-start | bytes 3538952 | tf_op jit(solution)/shard_map/ppermute | solution.py:111
  133.0 1.8 copy-start.2
Sparse Core Ops, SparseCore 0:
  35.1 97.8 all-gather.1

commit v2 on v1

v2 whole, which is shorter than its diff:
```python
import functools
import math

import jax
import jax.numpy as jnp
from jax import lax
from jax.experimental import pallas as pl
from jax.experimental.pallas import tpu as pltpu
from jax.sharding import PartitionSpec as P

TRANSPOSED = (((1,), (1,)), ((), ()))


def gate_of(timestep, mod_weight):
    width = mod_weight.shape[0]
    half_width = width // 2
    frequency = jnp.exp(-math.log(10000.0) * jnp.arange(half_width, dtype=jnp.float32) / half_width)
    angles = timestep.astype(jnp.float32) * frequency
    embedding = jnp.concatenate([jnp.cos(angles), jnp.sin(angles)])
    flat = mod_weight.reshape(width, -1)
    return jnp.dot(embedding[None, :], flat, precision=lax.Precision.HIGHEST)


def collect_kernel(own, up, across, down, quad, upper, lower):
    for place, block in enumerate((own, up, across, down)):
        quad[place] = block[...]
    upper[0] = own[...]
    upper[1] = up[...]
    lower[0] = down[...]
    lower[1] = own[...]


def collect(own, up, across, down):
    vmem = pl.BlockSpec(memory_space=pltpu.VMEM)
    shape = lambda count: jax.ShapeDtypeStruct((count,) + own.shape, own.dtype)
    return pl.pallas_call(
        collect_kernel,
        in_specs=[vmem] * 4,
        out_specs=[vmem] * 3,
        out_shape=[shape(4), shape(2), shape(2)],
        compiler_params=pltpu.CompilerParams(vmem_limit_bytes=16 * 2**20),
        cost_estimate=pl.CostEstimate(flops=10**11, bytes_accessed=8 * own.size, transcendentals=0),
    )(own, up, across, down)


def project_kernel(
    places_ref, quad, after, upper, lower, behind, weight_ref, near_ref, far_ref, rows_ref
):
    mine = places_ref[0]
    turn = places_ref[1]
    size = quad.shape[2]
    pieces = rows_ref.shape[0] // size
    weight = weight_ref[...]
    parts = [(quad, place, 4 * place) for place in range(4)]
    parts += [(after, place, 4 * place + 1) for place in range(4)]
    parts += [(upper, place, 4 * place + 2) for place in range(2)]
    parts += [(lower, place, 4 * place + 10) for place in range(2)]
    parts += [(behind, place, (4 * place + 15) % 16) for place in range(4)]
    for sample, out in ((1 - mine, far_ref), (mine, near_ref)):
        for part, place, offset in parts:
            at = pl.ds(pl.multiple_of(lax.rem(turn + offset, pieces) * size, size), size)
            rows_ref[at, :] = part[place, sample]
        out[...] = jnp.dot(rows_ref[...], weight, preferred_element_type=jnp.float32)


def project(places, parts, weight, sp):
    rows = sp * parts[0].shape[2]
    vmem = pl.BlockSpec(memory_space=pltpu.VMEM)
    return pl.pallas_call(
        project_kernel,
        in_specs=[pl.BlockSpec(memory_space=pltpu.SMEM)] + [vmem] * 6,
        out_specs=[vmem, vmem],
        out_shape=[jax.ShapeDtypeStruct((rows, weight.shape[1]), jnp.float32)] * 2,
        scratch_shapes=[pltpu.VMEM((rows, weight.shape[0]), jnp.bfloat16)],
        compiler_params=pltpu.CompilerParams(vmem_limit_bytes=24 * 2**20),
        cost_estimate=pl.CostEstimate(flops=10**11, bytes_accessed=2 * weight.size, transcendentals=0),
    )(places, *parts, weight)


def attend_kernel(
    length_ref, queries_ref, pairs_ref, near_ref, far_ref, gate_ref, image_out, text_out,
    keys_ref, values_ref, *, rows
):
    head = gate_ref.shape[1]
    text_count = near_ref.shape[0]
    scale = math.log2(math.e) / math.sqrt(head)
    text = (near_ref[...] + far_ref[...]).astype(jnp.bfloat16)
    keys_ref[:text_count, :] = text[:, head : 2 * head]
    keys_ref[text_count:, :] = pairs_ref[:, :head]
    values_ref[:text_count, :head] = text[:, 2 * head :]
    values_ref[text_count:, :head] = pairs_ref[:, head:]
    values_ref[:, head:] = jnp.ones((values_ref.shape[0], head), jnp.bfloat16)
    gate = gate_ref[...]
    position = lax.broadcasted_iota(jnp.int32, (1, text_count), 1)
    excluded = jnp.where(position < length_ref[0], 0.0, -jnp.inf)

    def one_block(queries):
        scores = lax.dot_general(
            queries, keys_ref[...], TRANSPOSED, preferred_element_type=jnp.float32
        )
        scores = jnp.concatenate(
            [scores[:, :text_count] + excluded, scores[:, text_count:]], axis=1
        )
        largest = jnp.max(scores, axis=-1, keepdims=True)
        weights = jnp.exp2((scores - largest) * scale).astype(jnp.bfloat16)
        total = jnp.dot(weights, values_ref[...], preferred_element_type=jnp.float32)
        return (total[:, :head] * (gate / total[:, head:])).astype(jnp.bfloat16)

    for block in range(queries_ref.shape[0] // rows):
        at = pl.ds(block * rows, rows)
        image_out[at, :] = one_block(queries_ref[at, :])
    text_out[...] = one_block(text[:, :head])


def attend(queries, pairs, near, far, length, gate_scale):
    image_count, head = queries.shape
    text_count = near.shape[0]
    keys = text_count + image_count
    vmem = pl.BlockSpec(memory_space=pltpu.VMEM)
    return pl.pallas_call(
        functools.partial(attend_kernel, rows=512),
        in_specs=[pl.BlockSpec(memory_space=pltpu.SMEM)] + [vmem] * 5,
        out_specs=[vmem, vmem],
        out_shape=[
            jax.ShapeDtypeStruct((image_count, head), jnp.bfloat16),
            jax.ShapeDtypeStruct((text_count, head), jnp.bfloat16),
        ],
        scratch_shapes=[
            pltpu.VMEM((keys, head), jnp.bfloat16),
            pltpu.VMEM((keys, 2 * head), jnp.bfloat16),
        ],
        compiler_params=pltpu.CompilerParams(vmem_limit_bytes=48 * 2**20),
    )(length, queries, pairs, near, far, gate_scale)


def shards(text_hidden, text_qkv_weight, image_qkv, mod_weight, lengths, timesteps):
    sec, sp, tp = (lax.axis_size(axis) for axis in ("sec", "sp", "tp"))
    mine = lax.axis_index("tp")
    head = mod_weight.shape[2]

    def ahead(x, by):
        return lax.ppermute(x, "sp", [((i + by) % sp, i) for i in range(sp)])

    def to_group(x, flip):
        moves = [
            (s * tp + t, ((s + sec // 2) % sec) * tp + (t + flip) % tp)
            for s in range(sec)
            for t in range(tp)
        ]
        return lax.ppermute(x, ("sec", "tp"), moves)

    across = ahead(text_hidden, 8)
    up = ahead(text_hidden, 4)
    down = ahead(text_hidden, -4)
    queries = image_qkv[0, :, :, :head].transpose(1, 0, 2)
    pairs = image_qkv[0, :, :, head:].transpose(1, 0, 2)
    queries = lax.all_to_all(queries, "sp", split_axis=0, concat_axis=0)
    heads, rows, _ = queries.shape
    gate_scale = gate_of(timesteps[0], mod_weight)

    quad, upper, lower = collect(text_hidden, up, across, down)
    after = ahead(quad, 1)
    behind = ahead(quad, -1)
    upper = ahead(upper, 2)
    lower = ahead(lower, -2)

    pairs, queries = lax.optimization_barrier((pairs, queries))
    pairs = lax.all_to_all(pairs, "sp", split_axis=0, concat_axis=0)

    places = jnp.stack([mine, lax.axis_index("sp")]).astype(jnp.int32)
    near, far = project(
        places, (quad, after, upper, lower, behind), text_qkv_weight[:, 0], sp
    )
    near = to_group(near, 0)
    far = to_group(far, 1)

    image_heads, text_out = attend(
        queries.reshape(heads * rows, head),
        pairs.reshape(heads * rows, 2 * head),
        near,
        far,
        lengths,
        gate_scale,
    )
    image_out = lax.all_to_all(
        image_heads.reshape(sp, rows, head), "sp", split_axis=0, concat_axis=0
    )
    return (image_out.transpose(1, 0, 2)[None], text_out[None, :, None, :])


def solution(mesh):
    in_specs = (
        P("sec", "sp", "tp"),
        P("tp", "sp", None),
        P(("sec", "tp"), "sp", None, None),
        P(None, "sp", None),
        P(("sec", "tp")),
        P(("sec", "tp")),
    )
    out_specs = (P(("sec", "tp"), "sp", None, None), P(("sec", "tp"), None, "sp", None))
    return jax.shard_map(shards, mesh=mesh, in_specs=in_specs, out_specs=out_specs, check_vma=False)
```

time: 187 us -> 169 us (0.904)
  the two profiles are of different devices: /device:TPU:12 before, /device:TPU:28 now
where the time goes in v2:
time: 169 us
  starting transfers between devices  62.2 us (37%)
  waiting for transfers between devices  56.4 us (33%)
  blocking collectives  33.2 us (20%)
  Pallas kernels  10.1 us (6%)
  local copies, waits for them, and re-layouts  4.49 us (3%)
  between operations  2.11 us (1%)
    ppermute x7, starting transfers between devices, ahead(): return lax.ppermute(x, 'sp', [((i + by) % sp, i) for i in range(sp)])  47.3 us
    all_to_all x1, blocking collectives, shards(): lax.all_to_all(image_heads.reshape(sp, rows, head), 'sp', split_axis=0, c...  33.2 us
    all_to_all x1, waiting for transfers between devices, shards(): pairs = lax.all_to_all(pairs, 'sp', split_axis=0, concat_axis=0)  27.1 us
    ppermute x7, waiting for transfers between devices, ahead(): return lax.ppermute(x, 'sp', [((i + by) % sp, i) for i in range(sp)])  14.5 us
    all_to_all x1, waiting for transfers between devices, shards(): queries = lax.all_to_all(queries, 'sp', split_axis=0, concat_axis=0)  7.74 us
    pallas_call x1, Pallas kernels, attend(): pl.pallas_call(functools.partial(attend_kernel, rows=512), in_specs=[pl.B...  7.03 us
    ppermute x2, waiting for transfers between devices, to_group(): return lax.ppermute(x, ('sec', 'tp'), moves)  7 us
    ppermute x2, starting transfers between devices, to_group(): return lax.ppermute(x, ('sec', 'tp'), moves)  5.62 us
  transfers between devices with their start and end apart: 11, of which 6 were waited for; matrix products, arithmetic and copies ran while one was open for 2% of the time, Pallas kernels for 2%

profile of v2, /device:TPU:28, one launch (start us, length us, event | category | flops | bytes accessed | tf_op | source)
XLA Modules:
  0.0 168.8 jit_solution(7235015627848307063)
XLA Ops:
  0.6 0.0 copy-start
  0.6 0.0 copy-start.2
  0.7 12.9 %collective-permute-start = (bf16[2,16,1536]{2,1,0:T(8,128)(2,1)}, bf16[2,16,1536]{2,1,0:T(8,128)(2,1)S(1)}, u32[]{:S(2)}, u32[]{:S(2)}) collective-permute-start(bf16[2,16,1536]{2,1,0:T(8,128)(2,1)} %own.1), channel_id=1, source_target_pairs={{8,0},{10,2},{12,4},{14,6},{16,8},{18,10},{20,12},{22,14},{24,16},... | collective-permute-start | bytes 294920 | tf_op jit(solution)/shard_map/ppermute | solution.py:142
  13.5 4.9 %collective-permute-start.1 = (bf16[2,16,1536]{2,1,0:T(8,128)(2,1)}, bf16[2,16,1536]{2,1,0:T(8,128)(2,1)S(1)}, u32[]{:S(2)}, u32[]{:S(2)}) collective-permute-start(bf16[2,16,1536]{2,1,0:T(8,128)(2,1)} %own.1), channel_id=1, source_target_pairs={{16,0},{18,2},{20,4},{22,6},{24,8},{26,10},{28,12},{30,14},{0,16},... | collective-permute-start | bytes 294920 | tf_op jit(solution)/shard_map/ppermute | solution.py:142
  18.4 7.8 %collective-permute-start.2 = (bf16[2,16,1536]{2,1,0:T(8,128)(2,1)}, bf16[2,16,1536]{2,1,0:T(8,128)(2,1)S(1)}, u32[]{:S(2)}, u32[]{:S(2)}) collective-permute-start(bf16[2,16,1536]{2,1,0:T(8,128)(2,1)} %own.1), channel_id=1, source_target_pairs={{24,0},{26,2},{28,4},{30,6},{0,8},{2,10},{4,12},{6,14},{8,16},{10,... | collective-permute-start | bytes 294920 | tf_op jit(solution)/shard_map/ppermute | solution.py:142
  26.3 1.1 slice.7
  27.4 0.9 copy.19
  28.3 5.1 %all-to-all-start = ((bf16[16,128,128]{2,1,0:T(8,128)(2,1)}), bf16[16,128,128]{2,1,0:T(8,128)(2,1)S(1)}, u32[]{:S(2)}, u32[]{:S(2)}) async-start(bf16[16,128,128]{2,1,0:T(8,128)(2,1)} %bitcast.25), calls=%async_computation | async-start | bytes 1048576 | tf_op jit(solution)/shard_map/all_to_all | solution.py:157
  33.4 0.0 collective-permute-done.up
  33.4 0.6 collective-permute-done.1.across
  34.0 0.0 collective-permute-done.2.down
  34.0 0.0 copy-done.2
  34.0 0.7 shard_map.77
  34.8 0.0 slice-start
  34.8 13.1 %collective-permute-start.3 = (bf16[4,2,16,1536]{3,2,1,0:T(8,128)(2,1)S(1)}, bf16[4,2,16,1536]{3,2,1,0:T(8,128)(2,1)}, u32[]{:S(2)}, u32[]{:S(2)}) collective-permute-start(bf16[4,2,16,1536]{3,2,1,0:T(8,128)(2,1)S(1)} %get-tuple-element.13.quad), channel_id=1, source_target_pairs={{2,0},{4,2},{6,4},{8,6},{10,8},{12,10},{14,12},{16,14},{18,16},{20... | collective-permute-start | bytes 1179656 | tf_op jit(solution)/shard_map/ppermute | solution.py:142
  47.9 1.9 %collective-permute-start.6 = (bf16[4,2,16,1536]{3,2,1,0:T(8,128)(2,1)S(1)}, bf16[4,2,16,1536]{3,2,1,0:T(8,128)(2,1)}, u32[]{:S(2)}, u32[]{:S(2)}) collective-permute-start(bf16[4,2,16,1536]{3,2,1,0:T(8,128)(2,1)S(1)} %get-tuple-element.13.quad), channel_id=1, source_target_pairs={{30,0},{0,2},{2,4},{4,6},{6,8},{8,10},{10,12},{12,14},{14,16},{16,... | collective-permute-start | bytes 1179656 | tf_op jit(solution)/shard_map/ppermute | solution.py:142
  49.8 3.4 %collective-permute-start.4 = (bf16[2,2,16,1536]{3,2,1,0:T(8,128)(2,1)}, bf16[2,2,16,1536]{3,2,1,0:T(8,128)(2,1)}, u32[]{:S(2)}, u32[]{:S(2)}) collective-permute-start(bf16[2,2,16,1536]{3,2,1,0:T(8,128)(2,1)} %get-tuple-element.14), channel_id=1, source_target_pairs={{4,0},{6,2},{8,4},{10,6},{12,8},{14,10},{16,12},{18,14},{20,16},{2... | collective-permute-start | bytes 589832 | tf_op jit(solution)/shard_map/ppermute | solution.py:142
  53.2 3.4 %collective-permute-start.5 = (bf16[2,2,16,1536]{3,2,1,0:T(8,128)(2,1)S(1)}, bf16[2,2,16,1536]{3,2,1,0:T(8,128)(2,1)}, u32[]{:S(2)}, u32[]{:S(2)}) collective-permute-start(bf16[2,2,16,1536]{3,2,1,0:T(8,128)(2,1)S(1)} %get-tuple-element.15), channel_id=1, source_target_pairs={{28,0},{30,2},{0,4},{2,6},{4,8},{6,10},{8,12},{10,14},{12,16},{14,... | collective-permute-start | bytes 589832 | tf_op jit(solution)/shard_map/ppermute | solution.py:142
  57.2 0.0 slice-done
  57.2 1.3 copy.18
  58.5 0.0 copy-start.1
  58.5 0.1 pad_add_fusion.places_ref
  58.6 7.7 %all-to-all-done = bf16[16,128,128]{2,1,0:T(8,128)(2,1)S(1)} async-done(((bf16[16,128,128]{2,1,0:T(8,128)(2,1)}), bf16[16,128,128]{2,1,0:T(8,128)(2,1)S(1)}, u32[]{:S(2)}, u32[]{:S(2)}) %all-to-all-start) | async-done | bytes 524320 | tf_op jit(solution)/shard_map/all_to_all | solution.py:157
  66.3 4.1 %all-to-all-start.1 = ((bf16[16,128,256]{2,1,0:T(8,128)(2,1)}), bf16[16,128,256]{2,1,0:T(8,128)(2,1)S(1)}, u32[]{:S(2)}, u32[]{:S(2)}) async-start(bf16[16,128,256]{2,1,0:T(8,128)(2,1)} %bitcast.31), calls=%async_computation.1 | async-start | bytes 2097152 | tf_op jit(solution)/shard_map/all_to_all | solution.py:168
  70.5 13.9 %collective-permute-done.4.upper = bf16[2,2,16,1536]{3,2,1,0:T(8,128)(2,1)} collective-permute-done((bf16[2,2,16,1536]{3,2,1,0:T(8,128)(2,1)}, bf16[2,2,16,1536]{3,2,1,0:T(8,128)(2,1)}, u32[]{:S(2)}, u32[]{:S(2)}) %collective-permute-start.4) | collective-permute-done | bytes 196640 | tf_op jit(solution)/shard_map/ppermute | solution.py:142
  84.4 0.0 collective-permute-done.5.lower
  84.4 0.0 collective-permute-done.3.after
  84.4 0.0 collective-permute-done.6.behind
  84.4 0.0 copy-done.1
  84.4 2.4 %shard_map.78 = (f32[256,384]{1,0:T(8,128)S(1)}, f32[256,384]{1,0:T(8,128)S(1)}) custom-call(s32[2]{0:T(128)S(1)} %pad_add_fusion.places_ref, bf16[4,2,16,1536]{3,2,1,0:T(8,128)(2,1)S(1)} %get-tuple-element.13.quad, bf16[4,2,16,1536]{3,2,1,0:T(8,128)(2,1)} %collective-permute-done.3.after, bf16[2,2,16,1536]{3,2,1,0:T(8,128)(2,1)} %collective-permute-done.4.upper, ...), custom_call_target="tpu_custom_call" | custom-call | flops 99999997952 | bytes 1179648 | tf_op jit(solution)/shard_map/pallas_call | solution.py:69
  86.8 2.7 %collective-permute-start.7 = (f32[256,384]{1,0:T(8,128)S(1)}, f32[256,384]{1,0:T(8,128)S(1)}, u32[]{:S(2)}, u32[]{:S(2)}) collective-permute-start(f32[256,384]{1,0:T(8,128)S(1)} %get-tuple-element.16), channel_id=1, source_target_pairs={{0,256},{1,257},{32,288},{33,289},{64,320},{65,321},{96,352},{97,3... | collective-permute-start | bytes 1179656 | tf_op jit(solution)/shard_map/ppermute | solution.py:150
  89.4 3.0 %collective-permute-start.8 = (f32[256,384]{1,0:T(8,128)S(1)}, f32[256,384]{1,0:T(8,128)S(1)}, u32[]{:S(2)}, u32[]{:S(2)}) collective-permute-start(f32[256,384]{1,0:T(8,128)S(1)} %get-tuple-element.17), channel_id=1, source_target_pairs={{0,257},{1,256},{32,289},{33,288},{64,321},{65,320},{96,353},{97,3... | collective-permute-start | bytes 1179656 | tf_op jit(solution)/shard_map/ppermute | solution.py:150
  92.4 0.1 fusion
  93.1 0.0 copy-done
  93.2 0.2 fusion.2.gate_ref
  93.3 3.1 %collective-permute-done.7.near_ref = f32[256,384]{1,0:T(8,128)S(1)} collective-permute-done((f32[256,384]{1,0:T(8,128)S(1)}, f32[256,384]{1,0:T(8,128)S(1)}, u32[]{:S(2)}, u32[]{:S(2)}) %collective-permute-start.7) | collective-permute-done | bytes 393248 | tf_op jit(solution)/shard_map/ppermute | solution.py:150
  96.5 3.9 %collective-permute-done.8.far_ref = f32[256,384]{1,0:T(8,128)S(1)} collective-permute-done((f32[256,384]{1,0:T(8,128)S(1)}, f32[256,384]{1,0:T(8,128)S(1)}, u32[]{:S(2)}, u32[]{:S(2)}) %collective-permute-start.8) | collective-permute-done | bytes 393248 | tf_op jit(solution)/shard_map/ppermute | solution.py:150
  100.3 27.1 %all-to-all-done.1 = bf16[16,128,256]{2,1,0:T(8,128)(2,1)S(1)} async-done(((bf16[16,128,256]{2,1,0:T(8,128)(2,1)}), bf16[16,128,256]{2,1,0:T(8,128)(2,1)S(1)}, u32[]{:S(2)}, u32[]{:S(2)}) %all-to-all-start.1) | async-done | bytes 1048608 | tf_op jit(solution)/shard_map/all_to_all | solution.py:168
  127.5 7.0 %shard_map.79 = (bf16[2048,128]{1,0:T(8,128)(2,1)S(1)}, bf16[256,128]{1,0:T(8,128)(2,1)}) custom-call(s32[1]{0:T(128)S(6)} %copy.20.length_ref, bf16[2048,128]{1,0:T(8,128)(2,1)S(1)} %bitcast.28, bf16[2048,256]{1,0:T(8,128)(2,1)S(1)} %bitcast.27, f32[256,384]{1,0:T(8,128)S(1)} %collective-permute-done.7.near_ref, ...), custom_call_target="tpu_custom_call" | custom-call | tf_op jit(solution)/shard_map/pallas_call | solution.py:120
  134.5 33.2 %all_to_all.15 = bf16[16,128,128]{2,1,0:T(8,128)(2,1)S(1)} all-to-all(bf16[16,128,128]{2,1,0:T(8,128)(2,1)S(1)} %bitcast.29), channel_id=1, replica_groups=mesh['sec'=16,'sp'=16,'tp'=2] {'sp'}, dimensions={0} | all-to-all | bytes 1048576 | tf_op jit(solution)/shard_map/all_to_all | solution.py:185
  167.7 1.1 copy.13
  (1 shorter events, 0.0 us)
Async XLA Ops:
  0.6 92.5 %copy-start = (f32[256,1,128]{2,1,0:T(1,128)S(1)}, f32[256,1,128]{2,1,0:T(1,128)}, u32[]{:S(2)}) copy-start(f32[256,1,128]{2,1,0:T(1,128)} %param.9) | copy-start | bytes 393220
  0.6 33.4 %copy-start.2 = (bf16[2,16,1536]{2,1,0:T(8,128)(2,1)S(1)}, bf16[2,16,1536]{2,1,0:T(8,128)(2,1)}, u32[]{:S(2)}) copy-start(bf16[2,16,1536]{2,1,0:T(8,128)(2,1)} %own.1) | copy-start | bytes 294916
  0.7 32.8 %collective-permute-start = (bf16[2,16,1536]{2,1,0:T(8,128)(2,1)}, bf16[2,16,1536]{2,1,0:T(8,128)(2,1)S(1)}, u32[]{:S(2)}, u32[]{:S(2)}) collective-permute-start(bf16[2,16,1536]{2,1,0:T(8,128)(2,1)} %own.1), channel_id=1, source_target_pairs={{8,0},{10,2},{12,4},{14,6},{16,8},{18,10},{20,12},{22,14},{24,16},... | collective-permute-start | bytes 294920 | tf_op jit(solution)/shard_map/ppermute | solution.py:142
  13.5 20.5 %collective-permute-start.1 = (bf16[2,16,1536]{2,1,0:T(8,128)(2,1)}, bf16[2,16,1536]{2,1,0:T(8,128)(2,1)S(1)}, u32[]{:S(2)}, u32[]{:S(2)}) collective-permute-start(bf16[2,16,1536]{2,1,0:T(8,128)(2,1)} %own.1), channel_id=1, source_target_pairs={{16,0},{18,2},{20,4},{22,6},{24,8},{26,10},{28,12},{30,14},{0,16},... | collective-permute-start | bytes 294920 | tf_op jit(solution)/shard_map/ppermute | solution.py:142
  18.4 15.6 %collective-permute-start.2 = (bf16[2,16,1536]{2,1,0:T(8,128)(2,1)}, bf16[2,16,1536]{2,1,0:T(8,128)(2,1)S(1)}, u32[]{:S(2)}, u32[]{:S(2)}) collective-permute-start(bf16[2,16,1536]{2,1,0:T(8,128)(2,1)} %own.1), channel_id=1, source_target_pairs={{24,0},{26,2},{28,4},{30,6},{0,8},{2,10},{4,12},{6,14},{8,16},{10,... | collective-permute-start | bytes 294920 | tf_op jit(solution)/shard_map/ppermute | solution.py:142
  28.3 38.1 %all-to-all-start = ((bf16[16,128,128]{2,1,0:T(8,128)(2,1)}), bf16[16,128,128]{2,1,0:T(8,128)(2,1)S(1)}, u32[]{:S(2)}, u32[]{:S(2)}) async-start(bf16[16,128,128]{2,1,0:T(8,128)(2,1)} %bitcast.25), calls=%async_computation | async-start | bytes 1048576 | tf_op jit(solution)/shard_map/all_to_all | solution.py:157
  34.8 22.4 %slice-start = ((bf16[1,128,16,384]{3,2,1,0:T(8,128)(2,1)}), bf16[1,128,16,256]{3,2,1,0:T(8,128)(2,1)S(1)}, s32[]{:S(2)}) async-start(bf16[1,128,16,384]{3,2,1,0:T(8,128)(2,1)} %param.8), calls=%async_computation.3 | async-start | bytes 2097152 | tf_op jit(solution)/shard_map/slice | solution.py:156
  34.8 49.6 %collective-permute-start.3 = (bf16[4,2,16,1536]{3,2,1,0:T(8,128)(2,1)S(1)}, bf16[4,2,16,1536]{3,2,1,0:T(8,128)(2,1)}, u32[]{:S(2)}, u32[]{:S(2)}) collective-permute-start(bf16[4,2,16,1536]{3,2,1,0:T(8,128)(2,1)S(1)} %get-tuple-element.13.quad), channel_id=1, source_target_pairs={{2,0},{4,2},{6,4},{8,6},{10,8},{12,10},{14,12},{16,14},{18,16},{20... | collective-permute-start | bytes 1179656 | tf_op jit(solution)/shard_map/ppermute | solution.py:142
  47.9 36.6 %collective-permute-start.6 = (bf16[4,2,16,1536]{3,2,1,0:T(8,128)(2,1)S(1)}, bf16[4,2,16,1536]{3,2,1,0:T(8,128)(2,1)}, u32[]{:S(2)}, u32[]{:S(2)}) collective-permute-start(bf16[4,2,16,1536]{3,2,1,0:T(8,128)(2,1)S(1)} %get-tuple-element.13.quad), channel_id=1, source_target_pairs={{30,0},{0,2},{2,4},{4,6},{6,8},{8,10},{10,12},{12,14},{14,16},{16,... | collective-permute-start | bytes 1179656 | tf_op jit(solution)/shard_map/ppermute | solution.py:142
  49.8 34.6 %collective-permute-start.4 = (bf16[2,2,16,1536]{3,2,1,0:T(8,128)(2,1)}, bf16[2,2,16,1536]{3,2,1,0:T(8,128)(2,1)}, u32[]{:S(2)}, u32[]{:S(2)}) collective-permute-start(bf16[2,2,16,1536]{3,2,1,0:T(8,128)(2,1)} %get-tuple-element.14), channel_id=1, source_target_pairs={{4,0},{6,2},{8,4},{10,6},{12,8},{14,10},{16,12},{18,14},{20,16},{2... | collective-permute-start | bytes 589832 | tf_op jit(solution)/shard_map/ppermute | solution.py:142
  53.2 31.2 %collective-permute-start.5 = (bf16[2,2,16,1536]{3,2,1,0:T(8,128)(2,1)S(1)}, bf16[2,2,16,1536]{3,2,1,0:T(8,128)(2,1)}, u32[]{:S(2)}, u32[]{:S(2)}) collective-permute-start(bf16[2,2,16,1536]{3,2,1,0:T(8,128)(2,1)S(1)} %get-tuple-element.15), channel_id=1, source_target_pairs={{28,0},{30,2},{0,4},{2,6},{4,8},{6,10},{8,12},{10,14},{12,16},{14,... | collective-permute-start | bytes 589832 | tf_op jit(solution)/shard_map/ppermute | solution.py:142
  58.5 25.9 %copy-start.1 = (bf16[1536,1,384]{2,0,1:T(8,128)(2,1)S(1)}, bf16[1536,1,384]{2,0,1:T(8,128)(2,1)}, u32[]{:S(2)}) copy-start(bf16[1536,1,384]{2,0,1:T(8,128)(2,1)} %param.7) | copy-start | bytes 3538948
  66.3 61.1 %all-to-all-start.1 = ((bf16[16,128,256]{2,1,0:T(8,128)(2,1)}), bf16[16,128,256]{2,1,0:T(8,128)(2,1)S(1)}, u32[]{:S(2)}, u32[]{:S(2)}) async-start(bf16[16,128,256]{2,1,0:T(8,128)(2,1)} %bitcast.31), calls=%async_computation.1 | async-start | bytes 2097152 | tf_op jit(solution)/shard_map/all_to_all | solution.py:168
  86.8 9.7 %collective-permute-start.7 = (f32[256,384]{1,0:T(8,128)S(1)}, f32[256,384]{1,0:T(8,128)S(1)}, u32[]{:S(2)}, u32[]{:S(2)}) collective-permute-start(f32[256,384]{1,0:T(8,128)S(1)} %get-tuple-element.16), channel_id=1, source_target_pairs={{0,256},{1,257},{32,288},{33,289},{64,320},{65,321},{96,352},{97,3... | collective-permute-start | bytes 1179656 | tf_op jit(solution)/shard_map/ppermute | solution.py:150
  89.4 10.9 %collective-permute-start.8 = (f32[256,384]{1,0:T(8,128)S(1)}, f32[256,384]{1,0:T(8,128)S(1)}, u32[]{:S(2)}, u32[]{:S(2)}) collective-permute-start(f32[256,384]{1,0:T(8,128)S(1)} %get-tuple-element.17), channel_id=1, source_target_pairs={{0,257},{1,256},{32,289},{33,288},{64,321},{65,320},{96,353},{97,3... | collective-permute-start | bytes 1179656 | tf_op jit(solution)/shard_map/ppermute | solution.py:150

commit v3 on v2

v3 whole, which is shorter than its diff:
```python
import functools
import math

import jax
import jax.numpy as jnp
from jax import lax
from jax.experimental import pallas as pl
from jax.experimental.pallas import tpu as pltpu
from jax.sharding import PartitionSpec as P

TRANSPOSED = (((1,), (1,)), ((), ()))


def gate_of(timestep, mod_weight):
    width = mod_weight.shape[0]
    half_width = width // 2
    frequency = jnp.exp(-math.log(10000.0) * jnp.arange(half_width, dtype=jnp.float32) / half_width)
    angles = timestep.astype(jnp.float32) * frequency
    embedding = jnp.concatenate([jnp.cos(angles), jnp.sin(angles)])
    flat = mod_weight.reshape(width, -1)
    return jnp.dot(embedding[None, :], flat, precision=lax.Precision.HIGHEST)


def collect_kernel(own, up, across, down, quad, upper, lower):
    for place, block in enumerate((own, up, across, down)):
        quad[place] = block[...]
    upper[0] = own[...]
    upper[1] = up[...]
    lower[0] = down[...]
    lower[1] = own[...]


def collect(own, up, across, down):
    vmem = pl.BlockSpec(memory_space=pltpu.VMEM)
    shape = lambda count: jax.ShapeDtypeStruct((count,) + own.shape, own.dtype)
    return pl.pallas_call(
        collect_kernel,
        in_specs=[vmem] * 4,
        out_specs=[vmem] * 3,
        out_shape=[shape(4), shape(2), shape(2)],
        compiler_params=pltpu.CompilerParams(vmem_limit_bytes=16 * 2**20),
        cost_estimate=pl.CostEstimate(flops=10**11, bytes_accessed=8 * own.size, transcendentals=0),
    )(own, up, across, down)


def project_kernel(
    turn_ref, quad, after, upper, lower, behind, own_weight, other_weight, out_ref, rows_ref
):
    size = quad.shape[1]
    half = own_weight.shape[0]
    pieces = rows_ref.shape[0] // size
    parts = [(quad, place, 4 * place) for place in range(4)]
    parts += [(after, place, 4 * place + 1) for place in range(4)]
    parts += [(upper, place, 4 * place + 2) for place in range(2)]
    parts += [(lower, place, 4 * place + 10) for place in range(2)]
    parts += [(behind, place, (4 * place + 15) % 16) for place in range(4)]
    for part, place, offset in parts:
        at = pl.ds(pl.multiple_of(lax.rem(turn_ref[0] + offset, pieces) * size, size), size)
        rows_ref[at, :] = part[place]
    total = jnp.dot(rows_ref[:, :half], own_weight[...], preferred_element_type=jnp.float32)
    total = total + jnp.dot(
        rows_ref[:, half:], other_weight[...], preferred_element_type=jnp.float32
    )
    out_ref[...] = total.astype(out_ref.dtype)


def project(turn, parts, own_weight, other_weight, sp):
    rows = sp * parts[0].shape[1]
    vmem = pl.BlockSpec(memory_space=pltpu.VMEM)
    return pl.pallas_call(
        project_kernel,
        in_specs=[pl.BlockSpec(memory_space=pltpu.SMEM)] + [vmem] * 7,
        out_specs=vmem,
        out_shape=jax.ShapeDtypeStruct((rows, own_weight.shape[1]), jnp.bfloat16),
        scratch_shapes=[pltpu.VMEM((rows, 2 * own_weight.shape[0]), jnp.bfloat16)],
        compiler_params=pltpu.CompilerParams(vmem_limit_bytes=24 * 2**20),
        cost_estimate=pl.CostEstimate(flops=10**11, bytes_accessed=10**6, transcendentals=0),
    )(turn, *parts, own_weight, other_weight)


def attender(length_ref, image_values, mixed_ref, text_ref, gate_ref, keys_ref, values_ref):
    text_count, width = text_ref.shape
    head = width // 3
    lines, rows, _ = image_values.shape
    scale = math.log2(math.e) / math.sqrt(head)
    keys_ref[:text_count, :] = text_ref[:, head : 2 * head]
    keys_ref[text_count:, :] = mixed_ref[:, :rows, :].reshape(lines * rows, head)
    values_ref[:text_count, :head] = text_ref[:, 2 * head :]
    values_ref[text_count:, :head] = image_values[...].reshape(lines * rows, head)
    values_ref[:, head:] = jnp.ones((values_ref.shape[0], head), jnp.bfloat16)
    gate = gate_ref[...]
    position = lax.broadcasted_iota(jnp.int32, (1, text_count), 1)
    excluded = jnp.where(position < length_ref[0], 0.0, -jnp.inf)

    def one_block(queries):
        scores = lax.dot_general(
            queries, keys_ref[...], TRANSPOSED, preferred_element_type=jnp.float32
        )
        scores = jnp.concatenate(
            [scores[:, :text_count] + excluded, scores[:, text_count:]], axis=1
        )
        largest = jnp.max(scores, axis=-1, keepdims=True)
        weights = jnp.exp2((scores - largest) * scale).astype(jnp.bfloat16)
        total = jnp.dot(weights, values_ref[...], preferred_element_type=jnp.float32)
        return (total[:, :head] * (gate / total[:, head:])).astype(jnp.bfloat16)

    return one_block


def early_kernel(
    length_ref, image_values, mixed_ref, text_ref, gate_ref, early_out, text_out, keys_ref, values_ref
):
    one_block = attender(
        length_ref, image_values, mixed_ref, text_ref, gate_ref, keys_ref, values_ref
    )
    lines, rows, head = early_out.shape
    first = mixed_ref.shape[1] - rows
    for line in range(0, lines, 8):
        queries = mixed_ref[line : line + 8, first:, :].reshape(8 * rows, head)
        early_out[line : line + 8] = one_block(queries).reshape(8, rows, head)
    text_out[...] = one_block(text_ref[:, :head])


def late_kernel(
    length_ref, image_values, mixed_ref, text_ref, gate_ref, late_ref, early_ref, image_out,
    keys_ref, values_ref
):
    one_block = attender(
        length_ref, image_values, mixed_ref, text_ref, gate_ref, keys_ref, values_ref
    )
    lines, rows, head = late_ref.shape
    half = early_ref.shape[1]
    image_out[:, :half, :] = early_ref[...]
    for line in range(0, lines, 8):
        queries = late_ref[line : line + 8].reshape(8 * rows, head)
        image_out[line : line + 8, half:, :] = one_block(queries).reshape(8, rows, head)


def attend(kernel, outs, length, values, mixed, text, gate_scale, *more):
    lines, rows, head = values.shape
    count = text.shape[0] + lines * rows
    vmem = pl.BlockSpec(memory_space=pltpu.VMEM)
    return pl.pallas_call(
        kernel,
        in_specs=[pl.BlockSpec(memory_space=pltpu.SMEM)] + [vmem] * (4 + len(more)),
        out_specs=[vmem] * len(outs),
        out_shape=[jax.ShapeDtypeStruct(shape, jnp.bfloat16) for shape in outs],
        scratch_shapes=[
            pltpu.VMEM((count, head), jnp.bfloat16),
            pltpu.VMEM((count, 2 * head), jnp.bfloat16),
        ],
        compiler_params=pltpu.CompilerParams(vmem_limit_bytes=40 * 2**20),
        cost_estimate=pl.CostEstimate(flops=10**9, bytes_accessed=10**6, transcendentals=0),
    )(length, values, mixed, text, gate_scale, *more)


def shards(text_hidden, text_qkv_weight, image_qkv, mod_weight, lengths, timesteps):
    sec, sp, tp = (lax.axis_size(axis) for axis in ("sec", "sp", "tp"))
    mine = lax.axis_index("tp")
    head = mod_weight.shape[2]

    def ahead(x, by):
        return lax.ppermute(x, "sp", [((i + by) % sp, i) for i in range(sp)])

    def to_group(x, flip):
        moves = [
            (s * tp + t, ((s + sec // 2) % sec) * tp + (t + flip) % tp)
            for s in range(sec)
            for t in range(tp)
        ]
        return lax.ppermute(x, ("sec", "tp"), moves)

    def to_heads(x):
        return lax.all_to_all(x, "sp", split_axis=0, concat_axis=0)

    half = image_qkv.shape[1] // 2
    keys = image_qkv[0, :, :, head : 2 * head].transpose(1, 0, 2)
    values = image_qkv[0, :, :, 2 * head :].transpose(1, 0, 2)
    early = image_qkv[0, :half, :, :head].transpose(1, 0, 2)
    late = image_qkv[0, half:, :, :head].transpose(1, 0, 2)
    mixed = to_heads(jnp.concatenate([keys, early], axis=1))

    near = to_group(lax.dynamic_index_in_dim(text_hidden, mine, 0, keepdims=False), 0)
    far = to_group(lax.dynamic_index_in_dim(text_hidden, 1 - mine, 0, keepdims=False), 1)
    own = jnp.concatenate([near, far], axis=1)
    own_weight = text_qkv_weight[:, 0]
    across = ahead(own, 8)
    up = ahead(own, 4)
    down = ahead(own, -4)
    values, mixed = lax.optimization_barrier((values, mixed))
    values = to_heads(values)
    gate_scale = gate_of(timesteps[0], mod_weight)

    quad, upper, lower = collect(own, up, across, down)
    after = ahead(quad, 1)
    behind = ahead(quad, -1)
    upper = ahead(upper, 2)
    lower = ahead(lower, -2)
    sent, quad = lax.optimization_barrier((own_weight, quad))
    other_weight = lax.ppermute(sent, "tp", [(0, 1), (1, 0)])
    late, values = lax.optimization_barrier((late, values))
    late = to_heads(late)

    turn = lax.axis_index("sp").astype(jnp.int32).reshape(1)
    text = project(turn, (quad, after, upper, lower, behind), own_weight, other_weight, sp)
    part = (sp, half, head)
    early, text_out = attend(
        early_kernel, (part, (text.shape[0], head)), lengths, values, mixed, text, gate_scale
    )
    (image_heads,) = attend(
        late_kernel, ((sp, 2 * half, head),), lengths, values, mixed, text, gate_scale, late, early
    )
    image_out = to_heads(image_heads)
    return (image_out.transpose(1, 0, 2)[None], text_out[None, :, None, :])


def solution(mesh):
    in_specs = (
        P("sec", "sp", "tp"),
        P("tp", "sp", None),
        P(("sec", "tp"), "sp", None, None),
        P(None, "sp", None),
        P(("sec", "tp")),
        P(("sec", "tp")),
    )
    out_specs = (P(("sec", "tp"), "sp", None, None), P(("sec", "tp"), None, "sp", None))
    return jax.shard_map(shards, mesh=mesh, in_specs=in_specs, out_specs=out_specs, check_vma=False)
```

time: 169 us -> 168 us (level)
  the two profiles are of different devices: /device:TPU:28 before, /device:TPU:30 now
where the time goes in v3:
time: 168 us; the launch traced here: 167 us
  starting transfers between devices  81.8 us (49%)
  blocking collectives  30 us (18%)
  waiting for transfers between devices  29.4 us (18%)
  Pallas kernels  11.6 us (7%)
  local copies, waits for them, and re-layouts  11 us (7%)
  between operations  2.18 us (1%)
    ppermute x7, starting transfers between devices, ahead(): return lax.ppermute(x, 'sp', [((i + by) % sp, i) for i in range(sp)])  40.2 us
    all_to_all x3, starting transfers between devices, to_heads(): return lax.all_to_all(x, 'sp', split_axis=0, concat_axis=0)  32.8 us
    all_to_all x1, blocking collectives, to_heads(): return lax.all_to_all(x, 'sp', split_axis=0, concat_axis=0)  30 us
    all_to_all x3, waiting for transfers between devices, to_heads(): return lax.all_to_all(x, 'sp', split_axis=0, concat_axis=0)  16.9 us
    pallas_call x2, Pallas kernels, attend(): pl.pallas_call(kernel, in_specs=[pl.BlockSpec(memory_space=pltpu.SMEM)] +...  8.76 us
    ppermute x7, waiting for transfers between devices, ahead(): return lax.ppermute(x, 'sp', [((i + by) % sp, i) for i in range(sp)])  8.27 us
    unnamed x22, local copies, waits for them, and re-layouts  7.76 us
    ppermute x2, starting transfers between devices, to_group(): return lax.ppermute(x, ('sec', 'tp'), moves)  5.62 us
  transfers between devices with their start and end apart: 13, of which 6 were waited for; matrix products, arithmetic and copies ran while one was open for 2% of the time, Pallas kernels for 4%

profile of v3, /device:TPU:30, one launch (start us, length us, event | category | flops | bytes accessed | tf_op | source)
XLA Modules:
  0.0 167.1 jit_solution(2305739783407784383)
XLA Ops:
  0.6 0.0 copy-start
  0.6 1.4 fusion.2
  2.1 1.8 %fusion.3 = (bf16[1,64,16,128]{3,2,1,0:T(8,128)(2,1)S(1)}, bf16[1,64,16,128]{3,2,1,0:T(8,128)(2,1)}) fusion(bf16[1,128,16,384]{3,2,1,0:T(8,128)(2,1)} %param.8), kind=kLoop, calls=%fused_computation.14 | loop fusion | bytes 1048576 | tf_op jit(solution)/shard_map/slice | solution.py:179
  3.8 0.1 copy.21
  4.0 0.1 copy.23
  4.0 0.0 copy-start.7
  4.1 1.0 pad_maximum_fusion
  5.0 15.2 %all-to-all-start = ((bf16[16,192,128]{2,1,0:T(8,128)(2,1)}), bf16[16,192,128]{2,1,0:T(8,128)(2,1)S(1)}, u32[]{:S(2)}, u32[]{:S(2)}) async-start(bf16[16,192,128]{2,1,0:T(8,128)(2,1)} %pad_maximum_fusion), calls=%async_computation | async-start | bytes 1572864 | tf_op jit(solution)/shard_map/all_to_all | solution.py:174
  20.2 0.0 copy-done.7
  20.3 2.7 %collective-permute-start = (bf16[16,1536]{1,0:T(8,128)(2,1)S(1)}, bf16[16,1536]{1,0:T(8,128)(2,1)S(1)}, u32[]{:S(2)}, u32[]{:S(2)}) collective-permute-start(bf16[16,1536]{1,0:T(8,128)(2,1)S(1)} %get-tuple-element.31), channel_id=1, source_target_pairs={{0,256},{1,257},{32,288},{33,289},{64,320},{65,321},{96,352},{97,3... | collective-permute-start | bytes 147464 | tf_op jit(solution)/shard_map/ppermute | solution.py:171
  22.9 3.0 %collective-permute-start.1 = (bf16[16,1536]{1,0:T(8,128)(2,1)S(1)}, bf16[16,1536]{1,0:T(8,128)(2,1)S(1)}, u32[]{:S(2)}, u32[]{:S(2)}) collective-permute-start(bf16[16,1536]{1,0:T(8,128)(2,1)S(1)} %get-tuple-element.30), channel_id=1, source_target_pairs={{0,257},{1,256},{32,289},{33,288},{64,321},{65,320},{96,353},{97,3... | collective-permute-start | bytes 147464 | tf_op jit(solution)/shard_map/ppermute | solution.py:171
  25.9 0.4 collective-permute-done
  26.2 3.9 %collective-permute-done.1 = bf16[16,1536]{1,0:T(8,128)(2,1)S(1)} collective-permute-done((bf16[16,1536]{1,0:T(8,128)(2,1)S(1)}, bf16[16,1536]{1,0:T(8,128)(2,1)S(1)}, u32[]{:S(2)}, u32[]{:S(2)}) %collective-permute-start.1) | collective-permute-done | bytes 49184 | tf_op jit(solution)/shard_map/ppermute | solution.py:171
  30.1 7.7 %collective-permute-start.2 = (bf16[16,3072]{1,0:T(8,128)(2,1)S(1)}, bf16[16,3072]{1,0:T(8,128)(2,1)S(1)}, u32[]{:S(2)}, u32[]{:S(2)}) collective-permute-start(bf16[16,3072]{1,0:T(8,128)(2,1)S(1)} %constant_dynamic-update-slice_fusion.own), channel_id=1, source_target_pairs={{8,0},{10,2},{12,4},{14,6},{16,8},{18,10},{20,12},{22,14},{24,16},... | collective-permute-start | bytes 294920 | tf_op jit(solution)/shard_map/ppermute | solution.py:163
  37.8 7.3 %collective-permute-start.3 = (bf16[16,3072]{1,0:T(8,128)(2,1)S(1)}, bf16[16,3072]{1,0:T(8,128)(2,1)S(1)}, u32[]{:S(2)}, u32[]{:S(2)}) collective-permute-start(bf16[16,3072]{1,0:T(8,128)(2,1)S(1)} %constant_dynamic-update-slice_fusion.own), channel_id=1, source_target_pairs={{16,0},{18,2},{20,4},{22,6},{24,8},{26,10},{28,12},{30,14},{0,16},... | collective-permute-start | bytes 294920 | tf_op jit(solution)/shard_map/ppermute | solution.py:163
  45.1 7.3 %collective-permute-start.4 = (bf16[16,3072]{1,0:T(8,128)(2,1)S(1)}, bf16[16,3072]{1,0:T(8,128)(2,1)S(1)}, u32[]{:S(2)}, u32[]{:S(2)}) collective-permute-start(bf16[16,3072]{1,0:T(8,128)(2,1)S(1)} %constant_dynamic-update-slice_fusion.own), channel_id=1, source_target_pairs={{24,0},{26,2},{28,4},{30,6},{0,8},{2,10},{4,12},{6,14},{8,16},{10,... | collective-permute-start | bytes 294920 | tf_op jit(solution)/shard_map/ppermute | solution.py:163
  52.4 0.9 copy.22
  53.4 11.5 %all-to-all-done.mixed_ref = bf16[16,192,128]{2,1,0:T(8,128)(2,1)S(1)} async-done(((bf16[16,192,128]{2,1,0:T(8,128)(2,1)}), bf16[16,192,128]{2,1,0:T(8,128)(2,1)S(1)}, u32[]{:S(2)}, u32[]{:S(2)}) %all-to-all-start) | async-done | bytes 786464 | tf_op jit(solution)/shard_map/all_to_all | solution.py:174
  64.8 7.3 %all-to-all-start.1 = ((bf16[16,128,128]{2,1,0:T(8,128)(2,1)}), bf16[16,128,128]{2,1,0:T(8,128)(2,1)S(1)}, u32[]{:S(2)}, u32[]{:S(2)}) async-start(bf16[16,128,128]{2,1,0:T(8,128)(2,1)} %bitcast.33), calls=%async_computation.1 | async-start | bytes 1048576 | tf_op jit(solution)/shard_map/all_to_all | solution.py:174
  72.1 0.0 copy-start.1
  72.1 0.0 collective-permute-done.2.up
  72.1 2.9 %collective-permute-done.3.across = bf16[16,3072]{1,0:T(8,128)(2,1)S(1)} collective-permute-done((bf16[16,3072]{1,0:T(8,128)(2,1)S(1)}, bf16[16,3072]{1,0:T(8,128)(2,1)S(1)}, u32[]{:S(2)}, u32[]{:S(2)}) %collective-permute-start.3) | collective-permute-done | bytes 98336 | tf_op jit(solution)/shard_map/ppermute | solution.py:163
  75.1 0.0 copy-start.3
  75.1 0.6 copy-done.3
  75.7 0.0 collective-permute-done.4.down
  75.7 0.0 copy-start.5
  75.7 0.6 copy-done.5
  76.3 0.0 copy-start.4
  76.3 0.9 copy-done.4
  77.2 0.0 copy-start.6
  77.2 0.9 copy-done.6
  78.1 0.1 shard_map.77
  78.2 0.0 copy-start.2
  78.2 0.7 copy-done.2
  78.9 0.0 copy-done.1
  78.9 3.1 %collective-permute-start.9 = (bf16[1536,384]{1,0:T(8,128)(2,1)S(1)}, bf16[1536,384]{1,0:T(8,128)(2,1)}, u32[]{:S(2)}, u32[]{:S(2)}) collective-permute-start(bf16[1536,384]{1,0:T(8,128)(2,1)S(1)} %bitcast.37), channel_id=1, source_target_pairs={{0,1},{1,0},{2,3},{3,2},{4,5},{5,4},{6,7},{7,6},{8,9},{9,8},{10,11... | collective-permute-start | bytes 3538952 | tf_op jit(solution)/shard_map/ppermute | solution.py:200
  82.7 3.3 %collective-permute-start.5 = (bf16[4,16,3072]{2,1,0:T(8,128)(2,1)S(1)}, bf16[4,16,3072]{2,1,0:T(8,128)(2,1)}, u32[]{:S(2)}, u32[]{:S(2)}) collective-permute-start(bf16[4,16,3072]{2,1,0:T(8,128)(2,1)S(1)} %get-tuple-element.17.quad), channel_id=1, source_target_pairs={{2,0},{4,2},{6,4},{8,6},{10,8},{12,10},{14,12},{16,14},{18,16},{20... | collective-permute-start | bytes 1179656 | tf_op jit(solution)/shard_map/ppermute | solution.py:163
  86.0 7.9 %collective-permute-start.8 = (bf16[4,16,3072]{2,1,0:T(8,128)(2,1)S(1)}, bf16[4,16,3072]{2,1,0:T(8,128)(2,1)}, u32[]{:S(2)}, u32[]{:S(2)}) collective-permute-start(bf16[4,16,3072]{2,1,0:T(8,128)(2,1)S(1)} %get-tuple-element.17.quad), channel_id=1, source_target_pairs={{30,0},{0,2},{2,4},{4,6},{6,8},{8,10},{10,12},{12,14},{14,16},{16,... | collective-permute-start | bytes 1179656 | tf_op jit(solution)/shard_map/ppermute | solution.py:163
  94.0 1.7 %copy.24 = bf16[1,64,16,128]{3,1,2,0:T(8,128)(2,1)} copy(bf16[1,64,16,128]{3,2,1,0:T(8,128)(2,1)} %get-tuple-element.29) | data formatting | bytes 524288
  96.3 2.1 %collective-permute-start.6 = (bf16[2,16,3072]{2,1,0:T(8,128)(2,1)}, bf16[2,16,3072]{2,1,0:T(8,128)(2,1)}, u32[]{:S(2)}, u32[]{:S(2)}) collective-permute-start(bf16[2,16,3072]{2,1,0:T(8,128)(2,1)} %copy-done.2), channel_id=1, source_target_pairs={{4,0},{6,2},{8,4},{10,6},{12,8},{14,10},{16,12},{18,14},{20,16},{2... | collective-permute-start | bytes 589832 | tf_op jit(solution)/shard_map/ppermute | solution.py:163
  98.5 4.6 %collective-permute-start.7 = (bf16[2,16,3072]{2,1,0:T(8,128)(2,1)S(1)}, bf16[2,16,3072]{2,1,0:T(8,128)(2,1)}, u32[]{:S(2)}, u32[]{:S(2)}) collective-permute-start(bf16[2,16,3072]{2,1,0:T(8,128)(2,1)S(1)} %get-tuple-element.19), channel_id=1, source_target_pairs={{28,0},{30,2},{0,4},{2,6},{4,8},{6,10},{8,12},{10,14},{12,16},{14,... | collective-permute-start | bytes 589832 | tf_op jit(solution)/shard_map/ppermute | solution.py:163
  103.1 0.0 copy-done
  103.1 0.2 fusion.4.gate_ref
  103.3 0.0 all-to-all-done.1.image_values
  103.3 10.3 %all-to-all-start.2 = ((bf16[16,64,128]{2,1,0:T(8,128)(2,1)}), bf16[16,64,128]{2,1,0:T(8,128)(2,1)S(1)}, u32[]{:S(2)}, u32[]{:S(2)}) async-start(bf16[16,64,128]{2,1,0:T(8,128)(2,1)} %bitcast.41), calls=%async_computation.2 | async-start | bytes 524288 | tf_op jit(solution)/shard_map/all_to_all | solution.py:174
  113.6 5.3 %collective-permute-done.6.upper = bf16[2,16,3072]{2,1,0:T(8,128)(2,1)} collective-permute-done((bf16[2,16,3072]{2,1,0:T(8,128)(2,1)}, bf16[2,16,3072]{2,1,0:T(8,128)(2,1)}, u32[]{:S(2)}, u32[]{:S(2)}) %collective-permute-start.6) | collective-permute-done | bytes 196640 | tf_op jit(solution)/shard_map/ppermute | solution.py:163
  119.0 0.0 collective-permute-done.7.lower
  119.0 0.0 collective-permute-done.5.after
  119.0 0.0 collective-permute-done.8.behind
  119.0 0.0 collective-permute-done.9.other_weight
  119.0 2.8 %shard_map.78.text_ref = bf16[256,384]{1,0:T(8,128)(2,1)S(1)} custom-call(s32[1]{0:T(128)} %bitcast.8.turn_ref, bf16[4,16,3072]{2,1,0:T(8,128)(2,1)S(1)} %get-tuple-element.17.quad, bf16[4,16,3072]{2,1,0:T(8,128)(2,1)} %collective-permute-done.5.after, bf16[2,16,3072]{2,1,0:T(8,128)(2,1)} %collective-permute-done.6.upper, ...), custom_call_target="tpu_custom_call" | custom-call | flops 99999997952 | bytes 1000000 | tf_op jit(solution)/shard_map/pallas_call | solution.py:70
  121.8 4.5 %shard_map.79 = (bf16[16,64,128]{2,1,0:T(8,128)(2,1)S(1)}, bf16[256,128]{1,0:T(8,128)(2,1)}) custom-call(s32[1]{0:T(128)S(6)} %copy.26.length_ref, bf16[16,128,128]{2,1,0:T(8,128)(2,1)S(1)} %all-to-all-done.1.image_values, bf16[16,192,128]{2,1,0:T(8,128)(2,1)S(1)} %all-to-all-done.mixed_ref, bf16[256,384]{1,0:T(8,128)(2,1)S(1)} %shard_map.78.text_ref, ...), custom_call_target="tpu_custom_call" | custom-call | flops 1000000000 | bytes 1000000 | tf_op jit(solution)/shard_map/pallas_call | solution.py:143
  126.3 5.4 %all-to-all-done.2.late_ref = bf16[16,64,128]{2,1,0:T(8,128)(2,1)S(1)} async-done(((bf16[16,64,128]{2,1,0:T(8,128)(2,1)}), bf16[16,64,128]{2,1,0:T(8,128)(2,1)S(1)}, u32[]{:S(2)}, u32[]{:S(2)}) %all-to-all-start.2) | async-done | bytes 262176 | tf_op jit(solution)/shard_map/all_to_all | solution.py:174
  131.7 4.3 %shard_map.80 = bf16[16,128,128]{2,1,0:T(8,128)(2,1)S(1)} custom-call(s32[1]{0:T(128)S(6)} %copy.26.length_ref, bf16[16,128,128]{2,1,0:T(8,128)(2,1)S(1)} %all-to-all-done.1.image_values, bf16[16,192,128]{2,1,0:T(8,128)(2,1)S(1)} %all-to-all-done.mixed_ref, bf16[256,384]{1,0:T(8,128)(2,1)S(1)} %shard_map.78.text_ref, f32[1,128]{1,0:T(1,128)S(1)} %fusion.4.gate_ref, ...), custom_call_target="tpu_custom_call" | custom-call | flops 1000000000 | bytes 1000000 | tf_op jit(solution)/shard_map/pallas_call | solution.py:143
  135.9 30.0 %all_to_all.20 = bf16[16,128,128]{2,1,0:T(8,128)(2,1)S(1)} all-to-all(bf16[16,128,128]{2,1,0:T(8,128)(2,1)S(1)} %shard_map.80), channel_id=1, replica_groups=mesh['sec'=16,'sp'=16,'tp'=2] {'sp'}, dimensions={0} | all-to-all | bytes 1048576 | tf_op jit(solution)/shard_map/all_to_all | solution.py:174
  165.9 1.1 copy.12
  (5 shorter events, 0.1 us)
Async XLA Ops:
  0.6 102.5 %copy-start = (f32[256,1,128]{2,1,0:T(1,128)S(1)}, f32[256,1,128]{2,1,0:T(1,128)}, u32[]{:S(2)}) copy-start(f32[256,1,128]{2,1,0:T(1,128)} %param.9) | copy-start | bytes 393220
  4.0 16.2 %copy-start.7 = (bf16[2,16,1536]{2,1,0:T(8,128)(2,1)S(1)}, bf16[2,16,1536]{2,1,0:T(8,128)(2,1)}, u32[]{:S(2)}) copy-start(bf16[2,16,1536]{2,1,0:T(8,128)(2,1)} %param.6) | copy-start | bytes 294916
  5.0 59.8 %all-to-all-start = ((bf16[16,192,128]{2,1,0:T(8,128)(2,1)}), bf16[16,192,128]{2,1,0:T(8,128)(2,1)S(1)}, u32[]{:S(2)}, u32[]{:S(2)}) async-start(bf16[16,192,128]{2,1,0:T(8,128)(2,1)} %pad_maximum_fusion), calls=%async_computation | async-start | bytes 1572864 | tf_op jit(solution)/shard_map/all_to_all | solution.py:174
  20.3 6.0 %collective-permute-start = (bf16[16,1536]{1,0:T(8,128)(2,1)S(1)}, bf16[16,1536]{1,0:T(8,128)(2,1)S(1)}, u32[]{:S(2)}, u32[]{:S(2)}) collective-permute-start(bf16[16,1536]{1,0:T(8,128)(2,1)S(1)} %get-tuple-element.31), channel_id=1, source_target_pairs={{0,256},{1,257},{32,288},{33,289},{64,320},{65,321},{96,352},{97,3... | collective-permute-start | bytes 147464 | tf_op jit(solution)/shard_map/ppermute | solution.py:171
  22.9 7.2 %collective-permute-start.1 = (bf16[16,1536]{1,0:T(8,128)(2,1)S(1)}, bf16[16,1536]{1,0:T(8,128)(2,1)S(1)}, u32[]{:S(2)}, u32[]{:S(2)}) collective-permute-start(bf16[16,1536]{1,0:T(8,128)(2,1)S(1)} %get-tuple-element.30), channel_id=1, source_target_pairs={{0,257},{1,256},{32,289},{33,288},{64,321},{65,320},{96,353},{97,3... | collective-permute-start | bytes 147464 | tf_op jit(solution)/shard_map/ppermute | solution.py:171
  30.1 42.0 %collective-permute-start.2 = (bf16[16,3072]{1,0:T(8,128)(2,1)S(1)}, bf16[16,3072]{1,0:T(8,128)(2,1)S(1)}, u32[]{:S(2)}, u32[]{:S(2)}) collective-permute-start(bf16[16,3072]{1,0:T(8,128)(2,1)S(1)} %constant_dynamic-update-slice_fusion.own), channel_id=1, source_target_pairs={{8,0},{10,2},{12,4},{14,6},{16,8},{18,10},{20,12},{22,14},{24,16},... | collective-permute-start | bytes 294920 | tf_op jit(solution)/shard_map/ppermute | solution.py:163
  37.8 37.2 %collective-permute-start.3 = (bf16[16,3072]{1,0:T(8,128)(2,1)S(1)}, bf16[16,3072]{1,0:T(8,128)(2,1)S(1)}, u32[]{:S(2)}, u32[]{:S(2)}) collective-permute-start(bf16[16,3072]{1,0:T(8,128)(2,1)S(1)} %constant_dynamic-update-slice_fusion.own), channel_id=1, source_target_pairs={{16,0},{18,2},{20,4},{22,6},{24,8},{26,10},{28,12},{30,14},{0,16},... | collective-permute-start | bytes 294920 | tf_op jit(solution)/shard_map/ppermute | solution.py:163
  45.1 30.6 %collective-permute-start.4 = (bf16[16,3072]{1,0:T(8,128)(2,1)S(1)}, bf16[16,3072]{1,0:T(8,128)(2,1)S(1)}, u32[]{:S(2)}, u32[]{:S(2)}) collective-permute-start(bf16[16,3072]{1,0:T(8,128)(2,1)S(1)} %constant_dynamic-update-slice_fusion.own), channel_id=1, source_target_pairs={{24,0},{26,2},{28,4},{30,6},{0,8},{2,10},{4,12},{6,14},{8,16},{10,... | collective-permute-start | bytes 294920 | tf_op jit(solution)/shard_map/ppermute | solution.py:163
  64.8 38.5 %all-to-all-start.1 = ((bf16[16,128,128]{2,1,0:T(8,128)(2,1)}), bf16[16,128,128]{2,1,0:T(8,128)(2,1)S(1)}, u32[]{:S(2)}, u32[]{:S(2)}) async-start(bf16[16,128,128]{2,1,0:T(8,128)(2,1)} %bitcast.33), calls=%async_computation.1 | async-start | bytes 1048576 | tf_op jit(solution)/shard_map/all_to_all | solution.py:174
  72.1 6.7 %copy-start.1 = (bf16[1536,1,384]{2,0,1:T(8,128)(2,1)S(1)}, bf16[1536,1,384]{2,0,1:T(8,128)(2,1)}, u32[]{:S(2)}) copy-start(bf16[1536,1,384]{2,0,1:T(8,128)(2,1)} %param.7) | copy-start | bytes 3538948
  75.1 0.6 copy-start.3
  75.7 0.6 copy-start.5
  76.3 0.9 copy-start.4
  77.2 0.9 copy-start.6
  78.2 0.7 copy-start.2
  78.9 40.1 %collective-permute-start.9 = (bf16[1536,384]{1,0:T(8,128)(2,1)S(1)}, bf16[1536,384]{1,0:T(8,128)(2,1)}, u32[]{:S(2)}, u32[]{:S(2)}) collective-permute-start(bf16[1536,384]{1,0:T(8,128)(2,1)S(1)} %bitcast.37), channel_id=1, source_target_pairs={{0,1},{1,0},{2,3},{3,2},{4,5},{5,4},{6,7},{7,6},{8,9},{9,8},{10,11... | collective-permute-start | bytes 3538952 | tf_op jit(solution)/shard_map/ppermute | solution.py:200
  82.7 36.3 %collective-permute-start.5 = (bf16[4,16,3072]{2,1,0:T(8,128)(2,1)S(1)}, bf16[4,16,3072]{2,1,0:T(8,128)(2,1)}, u32[]{:S(2)}, u32[]{:S(2)}) collective-permute-start(bf16[4,16,3072]{2,1,0:T(8,128)(2,1)S(1)} %get-tuple-element.17.quad), channel_id=1, source_target_pairs={{2,0},{4,2},{6,4},{8,6},{10,8},{12,10},{14,12},{16,14},{18,16},{20... | collective-permute-start | bytes 1179656 | tf_op jit(solution)/shard_map/ppermute | solution.py:163
  86.0 33.0 %collective-permute-start.8 = (bf16[4,16,3072]{2,1,0:T(8,128)(2,1)S(1)}, bf16[4,16,3072]{2,1,0:T(8,128)(2,1)}, u32[]{:S(2)}, u32[]{:S(2)}) collective-permute-start(bf16[4,16,3072]{2,1,0:T(8,128)(2,1)S(1)} %get-tuple-element.17.quad), channel_id=1, source_target_pairs={{30,0},{0,2},{2,4},{4,6},{6,8},{8,10},{10,12},{12,14},{14,16},{16,... | collective-permute-start | bytes 1179656 | tf_op jit(solution)/shard_map/ppermute | solution.py:163
  96.3 22.6 %collective-permute-start.6 = (bf16[2,16,3072]{2,1,0:T(8,128)(2,1)}, bf16[2,16,3072]{2,1,0:T(8,128)(2,1)}, u32[]{:S(2)}, u32[]{:S(2)}) collective-permute-start(bf16[2,16,3072]{2,1,0:T(8,128)(2,1)} %copy-done.2), channel_id=1, source_target_pairs={{4,0},{6,2},{8,4},{10,6},{12,8},{14,10},{16,12},{18,14},{20,16},{2... | collective-permute-start | bytes 589832 | tf_op jit(solution)/shard_map/ppermute | solution.py:163
  98.5 20.5 %collective-permute-start.7 = (bf16[2,16,3072]{2,1,0:T(8,128)(2,1)S(1)}, bf16[2,16,3072]{2,1,0:T(8,128)(2,1)}, u32[]{:S(2)}, u32[]{:S(2)}) collective-permute-start(bf16[2,16,3072]{2,1,0:T(8,128)(2,1)S(1)} %get-tuple-element.19), channel_id=1, source_target_pairs={{28,0},{30,2},{0,4},{2,6},{4,8},{6,10},{8,12},{10,14},{12,16},{14,... | collective-permute-start | bytes 589832 | tf_op jit(solution)/shard_map/ppermute | solution.py:163
  103.3 28.4 %all-to-all-start.2 = ((bf16[16,64,128]{2,1,0:T(8,128)(2,1)}), bf16[16,64,128]{2,1,0:T(8,128)(2,1)S(1)}, u32[]{:S(2)}, u32[]{:S(2)}) async-start(bf16[16,64,128]{2,1,0:T(8,128)(2,1)} %bitcast.41), calls=%async_computation.2 | async-start | bytes 524288 | tf_op jit(solution)/shard_map/all_to_all | solution.py:174

commit v4 on v3

--- a/solution.py
+++ b/solution.py
@@ -21,38 +21,32 @@
     return jnp.dot(embedding[None, :], flat, precision=lax.Precision.HIGHEST)
 
 
-def collect_kernel(own, up, across, down, quad, upper, lower):
+def collect_kernel(own, up, across, down, quad):
     for place, block in enumerate((own, up, across, down)):
         quad[place] = block[...]
-    upper[0] = own[...]
-    upper[1] = up[...]
-    lower[0] = down[...]
-    lower[1] = own[...]
 
 
 def collect(own, up, across, down):
     vmem = pl.BlockSpec(memory_space=pltpu.VMEM)
-    shape = lambda count: jax.ShapeDtypeStruct((count,) + own.shape, own.dtype)
     return pl.pallas_call(
         collect_kernel,
         in_specs=[vmem] * 4,
-        out_specs=[vmem] * 3,
-        out_shape=[shape(4), shape(2), shape(2)],
+        out_specs=vmem,
+        out_shape=jax.ShapeDtypeStruct((4,) + own.shape, own.dtype),
         compiler_params=pltpu.CompilerParams(vmem_limit_bytes=16 * 2**20),
-        cost_estimate=pl.CostEstimate(flops=10**11, bytes_accessed=8 * own.size, transcendentals=0),
+        cost_estimate=pl.CostEstimate(flops=10**11, bytes_accessed=10**6, transcendentals=0),
     )(own, up, across, down)
 
 
 def project_kernel(
-    turn_ref, quad, after, upper, lower, behind, own_weight, other_weight, out_ref, rows_ref
+    turn_ref, quad, after, middle, behind, own_weight, other_weight, out_ref, rows_ref
 ):
     size = quad.shape[1]
     half = own_weight.shape[0]
     pieces = rows_ref.shape[0] // size
     parts = [(quad, place, 4 * place) for place in range(4)]
     parts += [(after, place, 4 * place + 1) for place in range(4)]
-    parts += [(upper, place, 4 * place + 2) for place in range(2)]
-    parts += [(lower, place, 4 * place + 10) for place in range(2)]
+    parts += [(middle, place, 4 * place + turn_ref[1]) for place in range(4)]
     parts += [(behind, place, (4 * place + 15) % 16) for place in range(4)]
     for part, place, offset in parts:
         at = pl.ds(pl.multiple_of(lax.rem(turn_ref[0] + offset, pieces) * size, size), size)
@@ -69,7 +63,7 @@
     vmem = pl.BlockSpec(memory_space=pltpu.VMEM)
     return pl.pallas_call(
         project_kernel,
-        in_specs=[pl.BlockSpec(memory_space=pltpu.SMEM)] + [vmem] * 7,
+        in_specs=[pl.BlockSpec(memory_space=pltpu.SMEM)] + [vmem] * 6,
         out_specs=vmem,
         out_shape=jax.ShapeDtypeStruct((rows, own_weight.shape[1]), jnp.bfloat16),
         scratch_shapes=[pltpu.VMEM((rows, 2 * own_weight.shape[0]), jnp.bfloat16)],
@@ -191,18 +185,20 @@
     values = to_heads(values)
     gate_scale = gate_of(timesteps[0], mod_weight)
 
-    quad, upper, lower = collect(own, up, across, down)
+    quad = collect(own, up, across, down)
     after = ahead(quad, 1)
     behind = ahead(quad, -1)
-    upper = ahead(upper, 2)
-    lower = ahead(lower, -2)
+    apart = [2 if s % 2 == 0 else -2 for s in range(sec)]
+    moves = [(s * sp + (i + apart[s]) % sp, s * sp + i) for s in range(sec) for i in range(sp)]
+    middle = lax.ppermute(quad, ("sec", "sp"), moves)
     sent, quad = lax.optimization_barrier((own_weight, quad))
     other_weight = lax.ppermute(sent, "tp", [(0, 1), (1, 0)])
     late, values = lax.optimization_barrier((late, values))
     late = to_heads(late)
 
-    turn = lax.axis_index("sp").astype(jnp.int32).reshape(1)
-    text = project(turn, (quad, after, upper, lower, behind), own_weight, other_weight, sp)
+    shift = jnp.where(lax.axis_index("sec") % 2 == 0, 2, sp - 2)
+    turn = jnp.stack([lax.axis_index("sp"), shift]).astype(jnp.int32)
+    text = project(turn, (quad, after, middle, behind), own_weight, other_weight, sp)
     part = (sp, half, head)
     early, text_out = attend(
         early_kernel, (part, (text.shape[0], head)), lengths, values, mixed, text, gate_scale

time: 168 us -> 171 us (1.018)
  the two profiles are of different devices: /device:TPU:30 before, /device:TPU:28 now
where the time goes in v4:
time: 171 us; the launch traced here: 170 us
  starting transfers between devices  73.8 us (43%)
  waiting for transfers between devices  40.6 us (24%)
  blocking collectives  33.5 us (20%)
  Pallas kernels  11.6 us (7%)
  local copies, waits for them, and re-layouts  7.24 us (4%)
  between operations  2.17 us (1%)
    all_to_all x1, blocking collectives, to_heads(): return lax.all_to_all(x, 'sp', split_axis=0, concat_axis=0)  33.5 us
    ppermute x5, starting transfers between devices, ahead(): return lax.ppermute(x, 'sp', [((i + by) % sp, i) for i in range(sp)])  29.5 us
    all_to_all x3, starting transfers between devices, to_heads(): return lax.all_to_all(x, 'sp', split_axis=0, concat_axis=0)  29.4 us
    all_to_all x3, waiting for transfers between devices, to_heads(): return lax.all_to_all(x, 'sp', split_axis=0, concat_axis=0)  17.9 us
    ppermute x1, waiting for transfers between devices, shards(): middle = lax.ppermute(quad, ('sec', 'sp'), moves)  15.6 us
    pallas_call x2, Pallas kernels, attend(): pl.pallas_call(kernel, in_specs=[pl.BlockSpec(memory_space=pltpu.SMEM)] +...  8.84 us
    ppermute x1, starting transfers between devices, shards(): middle = lax.ppermute(quad, ('sec', 'sp'), moves)  6.11 us
    ppermute x2, starting transfers between devices, to_group(): return lax.ppermute(x, ('sec', 'tp'), moves)  5.62 us
  transfers between devices with their start and end apart: 12, of which 6 were waited for; matrix products, arithmetic and copies ran while one was open for 2% of the time, Pallas kernels for 4%

profile of v4, /device:TPU:28, one launch (start us, length us, event | category | flops | bytes accessed | tf_op | source)
XLA Modules:
  0.0 170.1 jit_solution(9963444470527474604)
XLA Ops:
  0.6 0.0 copy-start
  0.6 1.4 fusion.2
  2.1 1.8 %fusion.3 = (bf16[1,64,16,128]{3,2,1,0:T(8,128)(2,1)S(1)}, bf16[1,64,16,128]{3,2,1,0:T(8,128)(2,1)}) fusion(bf16[1,128,16,384]{3,2,1,0:T(8,128)(2,1)} %param.8), kind=kLoop, calls=%fused_computation.15 | loop fusion | bytes 1048576 | tf_op jit(solution)/shard_map/slice | solution.py:173
  3.8 0.1 copy.21
  4.0 0.1 copy.23
  4.0 0.0 copy-start.2
  4.1 1.0 pad_maximum_fusion
  5.0 15.2 %all-to-all-start = ((bf16[16,192,128]{2,1,0:T(8,128)(2,1)}), bf16[16,192,128]{2,1,0:T(8,128)(2,1)S(1)}, u32[]{:S(2)}, u32[]{:S(2)}) async-start(bf16[16,192,128]{2,1,0:T(8,128)(2,1)} %pad_maximum_fusion), calls=%async_computation | async-start | bytes 1572864 | tf_op jit(solution)/shard_map/all_to_all | solution.py:168
  20.2 0.0 copy-done.2
  20.3 2.7 %collective-permute-start = (bf16[16,1536]{1,0:T(8,128)(2,1)S(1)}, bf16[16,1536]{1,0:T(8,128)(2,1)S(1)}, u32[]{:S(2)}, u32[]{:S(2)}) collective-permute-start(bf16[16,1536]{1,0:T(8,128)(2,1)S(1)} %get-tuple-element.25), channel_id=1, source_target_pairs={{0,256},{1,257},{32,288},{33,289},{64,320},{65,321},{96,352},{97,3... | collective-permute-start | bytes 147464 | tf_op jit(solution)/shard_map/ppermute | solution.py:165
  22.9 3.0 %collective-permute-start.1 = (bf16[16,1536]{1,0:T(8,128)(2,1)S(1)}, bf16[16,1536]{1,0:T(8,128)(2,1)S(1)}, u32[]{:S(2)}, u32[]{:S(2)}) collective-permute-start(bf16[16,1536]{1,0:T(8,128)(2,1)S(1)} %get-tuple-element.24), channel_id=1, source_target_pairs={{0,257},{1,256},{32,289},{33,288},{64,321},{65,320},{96,353},{97,3... | collective-permute-start | bytes 147464 | tf_op jit(solution)/shard_map/ppermute | solution.py:165
  25.9 0.4 collective-permute-done
  26.2 3.9 %collective-permute-done.1 = bf16[16,1536]{1,0:T(8,128)(2,1)S(1)} collective-permute-done((bf16[16,1536]{1,0:T(8,128)(2,1)S(1)}, bf16[16,1536]{1,0:T(8,128)(2,1)S(1)}, u32[]{:S(2)}, u32[]{:S(2)}) %collective-permute-start.1) | collective-permute-done | bytes 49184 | tf_op jit(solution)/shard_map/ppermute | solution.py:165
  30.1 7.7 %collective-permute-start.2 = (bf16[16,3072]{1,0:T(8,128)(2,1)S(1)}, bf16[16,3072]{1,0:T(8,128)(2,1)S(1)}, u32[]{:S(2)}, u32[]{:S(2)}) collective-permute-start(bf16[16,3072]{1,0:T(8,128)(2,1)S(1)} %constant_dynamic-update-slice_fusion.own), channel_id=1, source_target_pairs={{8,0},{10,2},{12,4},{14,6},{16,8},{18,10},{20,12},{22,14},{24,16},... | collective-permute-start | bytes 294920 | tf_op jit(solution)/shard_map/ppermute | solution.py:157
  37.8 7.3 %collective-permute-start.3 = (bf16[16,3072]{1,0:T(8,128)(2,1)S(1)}, bf16[16,3072]{1,0:T(8,128)(2,1)S(1)}, u32[]{:S(2)}, u32[]{:S(2)}) collective-permute-start(bf16[16,3072]{1,0:T(8,128)(2,1)S(1)} %constant_dynamic-update-slice_fusion.own), channel_id=1, source_target_pairs={{16,0},{18,2},{20,4},{22,6},{24,8},{26,10},{28,12},{30,14},{0,16},... | collective-permute-start | bytes 294920 | tf_op jit(solution)/shard_map/ppermute | solution.py:157
  45.1 7.3 %collective-permute-start.4 = (bf16[16,3072]{1,0:T(8,128)(2,1)S(1)}, bf16[16,3072]{1,0:T(8,128)(2,1)S(1)}, u32[]{:S(2)}, u32[]{:S(2)}) collective-permute-start(bf16[16,3072]{1,0:T(8,128)(2,1)S(1)} %constant_dynamic-update-slice_fusion.own), channel_id=1, source_target_pairs={{24,0},{26,2},{28,4},{30,6},{0,8},{2,10},{4,12},{6,14},{8,16},{10,... | collective-permute-start | bytes 294920 | tf_op jit(solution)/shard_map/ppermute | solution.py:157
  52.4 0.9 copy.22
  53.3 11.5 %all-to-all-done.mixed_ref = bf16[16,192,128]{2,1,0:T(8,128)(2,1)S(1)} async-done(((bf16[16,192,128]{2,1,0:T(8,128)(2,1)}), bf16[16,192,128]{2,1,0:T(8,128)(2,1)S(1)}, u32[]{:S(2)}, u32[]{:S(2)}) %all-to-all-start) | async-done | bytes 786464 | tf_op jit(solution)/shard_map/all_to_all | solution.py:168
  64.8 7.3 %all-to-all-start.1 = ((bf16[16,128,128]{2,1,0:T(8,128)(2,1)}), bf16[16,128,128]{2,1,0:T(8,128)(2,1)S(1)}, u32[]{:S(2)}, u32[]{:S(2)}) async-start(bf16[16,128,128]{2,1,0:T(8,128)(2,1)} %bitcast.34), calls=%async_computation.1 | async-start | bytes 1048576 | tf_op jit(solution)/shard_map/all_to_all | solution.py:168
  72.1 0.0 copy-start.1
  72.1 0.0 collective-permute-done.2.up
  72.1 2.9 %collective-permute-done.3.across = bf16[16,3072]{1,0:T(8,128)(2,1)S(1)} collective-permute-done((bf16[16,3072]{1,0:T(8,128)(2,1)S(1)}, bf16[16,3072]{1,0:T(8,128)(2,1)S(1)}, u32[]{:S(2)}, u32[]{:S(2)}) %collective-permute-start.3) | collective-permute-done | bytes 98336 | tf_op jit(solution)/shard_map/ppermute | solution.py:157
  75.1 0.0 collective-permute-done.4.down
  75.1 0.0 copy-done.1
  75.1 3.1 %collective-permute-start.8 = (bf16[1536,384]{1,0:T(8,128)(2,1)S(1)}, bf16[1536,384]{1,0:T(8,128)(2,1)}, u32[]{:S(2)}, u32[]{:S(2)}) collective-permute-start(bf16[1536,384]{1,0:T(8,128)(2,1)S(1)} %bitcast.38), channel_id=1, source_target_pairs={{0,1},{1,0},{2,3},{3,2},{4,5},{5,4},{6,7},{7,6},{8,9},{9,8},{10,11... | collective-permute-start | bytes 3538952 | tf_op jit(solution)/shard_map/ppermute | solution.py:195
  79.0 3.3 %collective-permute-start.5 = (bf16[4,16,3072]{2,1,0:T(8,128)(2,1)S(1)}, bf16[4,16,3072]{2,1,0:T(8,128)(2,1)}, u32[]{:S(2)}, u32[]{:S(2)}) collective-permute-start(bf16[4,16,3072]{2,1,0:T(8,128)(2,1)S(1)} %shard_map.77.quad), channel_id=1, source_target_pairs={{2,0},{4,2},{6,4},{8,6},{10,8},{12,10},{14,12},{16,14},{18,16},{20... | collective-permute-start | bytes 1179656 | tf_op jit(solution)/shard_map/ppermute | solution.py:157
  82.3 6.1 %collective-permute-start.6 = (bf16[4,16,3072]{2,1,0:T(8,128)(2,1)S(1)}, bf16[4,16,3072]{2,1,0:T(8,128)(2,1)}, u32[]{:S(2)}, u32[]{:S(2)}) collective-permute-start(bf16[4,16,3072]{2,1,0:T(8,128)(2,1)S(1)} %shard_map.77.quad), channel_id=1, source_target_pairs={{4,0},{6,2},{8,4},{10,6},{12,8},{14,10},{16,12},{18,14},{20,16},{2... | collective-permute-start | bytes 1179656 | tf_op jit(solution)/shard_map/ppermute | solution.py:193
  88.4 3.9 %collective-permute-start.7 = (bf16[4,16,3072]{2,1,0:T(8,128)(2,1)S(1)}, bf16[4,16,3072]{2,1,0:T(8,128)(2,1)}, u32[]{:S(2)}, u32[]{:S(2)}) collective-permute-start(bf16[4,16,3072]{2,1,0:T(8,128)(2,1)S(1)} %shard_map.77.quad), channel_id=1, source_target_pairs={{30,0},{0,2},{2,4},{4,6},{6,8},{8,10},{10,12},{12,14},{14,16},{16,... | collective-permute-start | bytes 1179656 | tf_op jit(solution)/shard_map/ppermute | solution.py:157
  92.4 0.1 pad_add_fusion.turn_ref
  92.4 1.7 %copy.24 = bf16[1,64,16,128]{3,1,2,0:T(8,128)(2,1)} copy(bf16[1,64,16,128]{3,2,1,0:T(8,128)(2,1)} %get-tuple-element.23) | data formatting | bytes 524288
  94.8 0.0 copy-done
  94.9 0.2 fusion.4.gate_ref
  95.0 6.4 %all-to-all-done.1.image_values = bf16[16,128,128]{2,1,0:T(8,128)(2,1)S(1)} async-done(((bf16[16,128,128]{2,1,0:T(8,128)(2,1)}), bf16[16,128,128]{2,1,0:T(8,128)(2,1)S(1)}, u32[]{:S(2)}, u32[]{:S(2)}) %all-to-all-start.1) | async-done | bytes 524320 | tf_op jit(solution)/shard_map/all_to_all | solution.py:168
  101.4 6.9 %all-to-all-start.2 = ((bf16[16,64,128]{2,1,0:T(8,128)(2,1)}), bf16[16,64,128]{2,1,0:T(8,128)(2,1)S(1)}, u32[]{:S(2)}, u32[]{:S(2)}) async-start(bf16[16,64,128]{2,1,0:T(8,128)(2,1)} %bitcast.36), calls=%async_computation.2 | async-start | bytes 524288 | tf_op jit(solution)/shard_map/all_to_all | solution.py:168
  108.3 0.0 collective-permute-done.5.after
  108.3 15.6 %collective-permute-done.6.middle = bf16[4,16,3072]{2,1,0:T(8,128)(2,1)} collective-permute-done((bf16[4,16,3072]{2,1,0:T(8,128)(2,1)S(1)}, bf16[4,16,3072]{2,1,0:T(8,128)(2,1)}, u32[]{:S(2)}, u32[]{:S(2)}) %collective-permute-start.6) | collective-permute-done | bytes 393248 | tf_op jit(solution)/shard_map/ppermute | solution.py:193
  123.9 0.0 collective-permute-done.7.behind
  123.9 0.0 collective-permute-done.8.other_weight
  123.9 2.7 %shard_map.78.text_ref = bf16[256,384]{1,0:T(8,128)(2,1)S(1)} custom-call(s32[2]{0:T(128)S(1)} %pad_add_fusion.turn_ref, bf16[4,16,3072]{2,1,0:T(8,128)(2,1)S(1)} %shard_map.77.quad, bf16[4,16,3072]{2,1,0:T(8,128)(2,1)} %collective-permute-done.5.after, bf16[4,16,3072]{2,1,0:T(8,128)(2,1)} %collective-permute-done.6.middle, ...), custom_call_target="tpu_custom_call" | custom-call | flops 99999997952 | bytes 1000000 | tf_op jit(solution)/shard_map/pallas_call | solution.py:64
  126.7 4.6 %shard_map.79 = (bf16[16,64,128]{2,1,0:T(8,128)(2,1)S(1)}, bf16[256,128]{1,0:T(8,128)(2,1)}) custom-call(s32[1]{0:T(128)S(6)} %copy.26.length_ref, bf16[16,128,128]{2,1,0:T(8,128)(2,1)S(1)} %all-to-all-done.1.image_values, bf16[16,192,128]{2,1,0:T(8,128)(2,1)S(1)} %all-to-all-done.mixed_ref, bf16[256,384]{1,0:T(8,128)(2,1)S(1)} %shard_map.78.text_ref, ...), custom_call_target="tpu_custom_call" | custom-call | flops 1000000000 | bytes 1000000 | tf_op jit(solution)/shard_map/pallas_call | solution.py:137
  131.2 0.0 all-to-all-done.2.late_ref
  131.2 4.3 %shard_map.80 = bf16[16,128,128]{2,1,0:T(8,128)(2,1)S(1)} custom-call(s32[1]{0:T(128)S(6)} %copy.26.length_ref, bf16[16,128,128]{2,1,0:T(8,128)(2,1)S(1)} %all-to-all-done.1.image_values, bf16[16,192,128]{2,1,0:T(8,128)(2,1)S(1)} %all-to-all-done.mixed_ref, bf16[256,384]{1,0:T(8,128)(2,1)S(1)} %shard_map.78.text_ref, f32[1,128]{1,0:T(1,128)S(1)} %fusion.4.gate_ref, ...), custom_call_target="tpu_custom_call" | custom-call | flops 1000000000 | bytes 1000000 | tf_op jit(solution)/shard_map/pallas_call | solution.py:137
  135.5 33.5 %all_to_all.20 = bf16[16,128,128]{2,1,0:T(8,128)(2,1)S(1)} all-to-all(bf16[16,128,128]{2,1,0:T(8,128)(2,1)S(1)} %shard_map.80), channel_id=1, replica_groups=mesh['sec'=16,'sp'=16,'tp'=2] {'sp'}, dimensions={0} | all-to-all | bytes 1048576 | tf_op jit(solution)/shard_map/all_to_all | solution.py:168
  169.0 1.1 copy.12
  (6 shorter events, 0.1 us)
Async XLA Ops:
  0.6 94.2 %copy-start = (f32[256,1,128]{2,1,0:T(1,128)S(1)}, f32[256,1,128]{2,1,0:T(1,128)}, u32[]{:S(2)}) copy-start(f32[256,1,128]{2,1,0:T(1,128)} %param.9) | copy-start | bytes 393220
  4.0 16.2 %copy-start.2 = (bf16[2,16,1536]{2,1,0:T(8,128)(2,1)S(1)}, bf16[2,16,1536]{2,1,0:T(8,128)(2,1)}, u32[]{:S(2)}) copy-start(bf16[2,16,1536]{2,1,0:T(8,128)(2,1)} %param.6) | copy-start | bytes 294916
  5.0 59.8 %all-to-all-start = ((bf16[16,192,128]{2,1,0:T(8,128)(2,1)}), bf16[16,192,128]{2,1,0:T(8,128)(2,1)S(1)}, u32[]{:S(2)}, u32[]{:S(2)}) async-start(bf16[16,192,128]{2,1,0:T(8,128)(2,1)} %pad_maximum_fusion), calls=%async_computation | async-start | bytes 1572864 | tf_op jit(solution)/shard_map/all_to_all | solution.py:168
  20.3 6.0 %collective-permute-start = (bf16[16,1536]{1,0:T(8,128)(2,1)S(1)}, bf16[16,1536]{1,0:T(8,128)(2,1)S(1)}, u32[]{:S(2)}, u32[]{:S(2)}) collective-permute-start(bf16[16,1536]{1,0:T(8,128)(2,1)S(1)} %get-tuple-element.25), channel_id=1, source_target_pairs={{0,256},{1,257},{32,288},{33,289},{64,320},{65,321},{96,352},{97,3... | collective-permute-start | bytes 147464 | tf_op jit(solution)/shard_map/ppermute | solution.py:165
  22.9 7.2 %collective-permute-start.1 = (bf16[16,1536]{1,0:T(8,128)(2,1)S(1)}, bf16[16,1536]{1,0:T(8,128)(2,1)S(1)}, u32[]{:S(2)}, u32[]{:S(2)}) collective-permute-start(bf16[16,1536]{1,0:T(8,128)(2,1)S(1)} %get-tuple-element.24), channel_id=1, source_target_pairs={{0,257},{1,256},{32,289},{33,288},{64,321},{65,320},{96,353},{97,3... | collective-permute-start | bytes 147464 | tf_op jit(solution)/shard_map/ppermute | solution.py:165
  30.1 42.0 %collective-permute-start.2 = (bf16[16,3072]{1,0:T(8,128)(2,1)S(1)}, bf16[16,3072]{1,0:T(8,128)(2,1)S(1)}, u32[]{:S(2)}, u32[]{:S(2)}) collective-permute-start(bf16[16,3072]{1,0:T(8,128)(2,1)S(1)} %constant_dynamic-update-slice_fusion.own), channel_id=1, source_target_pairs={{8,0},{10,2},{12,4},{14,6},{16,8},{18,10},{20,12},{22,14},{24,16},... | collective-permute-start | bytes 294920 | tf_op jit(solution)/shard_map/ppermute | solution.py:157
  37.8 37.2 %collective-permute-start.3 = (bf16[16,3072]{1,0:T(8,128)(2,1)S(1)}, bf16[16,3072]{1,0:T(8,128)(2,1)S(1)}, u32[]{:S(2)}, u32[]{:S(2)}) collective-permute-start(bf16[16,3072]{1,0:T(8,128)(2,1)S(1)} %constant_dynamic-update-slice_fusion.own), channel_id=1, source_target_pairs={{16,0},{18,2},{20,4},{22,6},{24,8},{26,10},{28,12},{30,14},{0,16},... | collective-permute-start | bytes 294920 | tf_op jit(solution)/shard_map/ppermute | solution.py:157
  45.1 29.9 %collective-permute-start.4 = (bf16[16,3072]{1,0:T(8,128)(2,1)S(1)}, bf16[16,3072]{1,0:T(8,128)(2,1)S(1)}, u32[]{:S(2)}, u32[]{:S(2)}) collective-permute-start(bf16[16,3072]{1,0:T(8,128)(2,1)S(1)} %constant_dynamic-update-slice_fusion.own), channel_id=1, source_target_pairs={{24,0},{26,2},{28,4},{30,6},{0,8},{2,10},{4,12},{6,14},{8,16},{10,... | collective-permute-start | bytes 294920 | tf_op jit(solution)/shard_map/ppermute | solution.py:157
  64.8 36.6 %all-to-all-start.1 = ((bf16[16,128,128]{2,1,0:T(8,128)(2,1)}), bf16[16,128,128]{2,1,0:T(8,128)(2,1)S(1)}, u32[]{:S(2)}, u32[]{:S(2)}) async-start(bf16[16,128,128]{2,1,0:T(8,128)(2,1)} %bitcast.34), calls=%async_computation.1 | async-start | bytes 1048576 | tf_op jit(solution)/shard_map/all_to_all | solution.py:168
  72.1 3.0 %copy-start.1 = (bf16[1536,1,384]{2,0,1:T(8,128)(2,1)S(1)}, bf16[1536,1,384]{2,0,1:T(8,128)(2,1)}, u32[]{:S(2)}) copy-start(bf16[1536,1,384]{2,0,1:T(8,128)(2,1)} %param.7) | copy-start | bytes 3538948
  75.1 48.8 %collective-permute-start.8 = (bf16[1536,384]{1,0:T(8,128)(2,1)S(1)}, bf16[1536,384]{1,0:T(8,128)(2,1)}, u32[]{:S(2)}, u32[]{:S(2)}) collective-permute-start(bf16[1536,384]{1,0:T(8,128)(2,1)S(1)} %bitcast.38), channel_id=1, source_target_pairs={{0,1},{1,0},{2,3},{3,2},{4,5},{5,4},{6,7},{7,6},{8,9},{9,8},{10,11... | collective-permute-start | bytes 3538952 | tf_op jit(solution)/shard_map/ppermute | solution.py:195
  79.0 29.4 %collective-permute-start.5 = (bf16[4,16,3072]{2,1,0:T(8,128)(2,1)S(1)}, bf16[4,16,3072]{2,1,0:T(8,128)(2,1)}, u32[]{:S(2)}, u32[]{:S(2)}) collective-permute-start(bf16[4,16,3072]{2,1,0:T(8,128)(2,1)S(1)} %shard_map.77.quad), channel_id=1, source_target_pairs={{2,0},{4,2},{6,4},{8,6},{10,8},{12,10},{14,12},{16,14},{18,16},{20... | collective-permute-start | bytes 1179656 | tf_op jit(solution)/shard_map/ppermute | solution.py:157
  82.3 41.6 %collective-permute-start.6 = (bf16[4,16,3072]{2,1,0:T(8,128)(2,1)S(1)}, bf16[4,16,3072]{2,1,0:T(8,128)(2,1)}, u32[]{:S(2)}, u32[]{:S(2)}) collective-permute-start(bf16[4,16,3072]{2,1,0:T(8,128)(2,1)S(1)} %shard_map.77.quad), channel_id=1, source_target_pairs={{4,0},{6,2},{8,4},{10,6},{12,8},{14,10},{16,12},{18,14},{20,16},{2... | collective-permute-start | bytes 1179656 | tf_op jit(solution)/shard_map/ppermute | solution.py:193
  88.4 35.5 %collective-permute-start.7 = (bf16[4,16,3072]{2,1,0:T(8,128)(2,1)S(1)}, bf16[4,16,3072]{2,1,0:T(8,128)(2,1)}, u32[]{:S(2)}, u32[]{:S(2)}) collective-permute-start(bf16[4,16,3072]{2,1,0:T(8,128)(2,1)S(1)} %shard_map.77.quad), channel_id=1, source_target_pairs={{30,0},{0,2},{2,4},{4,6},{6,8},{8,10},{10,12},{12,14},{14,16},{16,... | collective-permute-start | bytes 1179656 | tf_op jit(solution)/shard_map/ppermute | solution.py:157
  101.4 29.8 %all-to-all-start.2 = ((bf16[16,64,128]{2,1,0:T(8,128)(2,1)}), bf16[16,64,128]{2,1,0:T(8,128)(2,1)S(1)}, u32[]{:S(2)}, u32[]{:S(2)}) async-start(bf16[16,64,128]{2,1,0:T(8,128)(2,1)} %bitcast.36), calls=%async_computation.2 | async-start | bytes 524288 | tf_op jit(solution)/shard_map/all_to_all | solution.py:168
